TPU v7x, 32 devices: a whole 2x2x4 slice. The times are simulated.
32 devices in a mesh: expert: 8 (over y, x, core), fsdp: 4 (over z).
Axes of the slice: x: 2, y: 2, z: 4, core: 2. Of those that a mesh axis runs over, the one named last changes fastest.
Arguments:
- tokens: bfloat16 [1024, 7168], P('expert', 'fsdp'), may hold values from -6 to 6
- counts: int32 [8, 4], P('expert'), may hold values from 1 to 64, as said below
- gate_values: bfloat16 [8, 7168, 1024], P('expert', 'fsdp'), may hold values from -0.0625 to 0.0625
- up_values: bfloat16 [8, 7168, 1024], P('expert', 'fsdp'), may hold values from -0.0625 to 0.0625
- gate_scales: float32 [8, 56, 8], P('expert'), may hold values from 0.5 to 2
- up_scales: float32 [8, 56, 8], P('expert'), may hold values from 0.5 to 2
- grad_hidden: bfloat16 [8, 512, 1024], P('expert', 'fsdp'), may hold values from -6 to 6
Outputs:
- hidden: bfloat16 [8, 512, 1024], P('expert', 'fsdp')
- grad_gate: bfloat16 [8, 7168, 1024], P('expert', 'fsdp')
- grad_up: bfloat16 [8, 7168, 1024], P('expert', 'fsdp')
- grad_tokens: bfloat16 [1024, 7168], P('expert', 'fsdp')
Inputs may be any that keep to these rules, and one draw needn't show every extreme that they name: Each row of counts sums to 128. In every draw one expert, drawn from the seed, receives exactly 64 rows from every source index.
All inputs are finite; a program needn't handle non-finite values.
Results may differ from a plain program's by a relative error of at most 0.025.
Values may be sent and summed in bfloat16 or wider, within the bound.
No kernel may reach another device: no remote copies, remote signals or barrier semaphores. Data moves between devices by JAX's collectives and lax.ppermute only.
A program may use at most 64 MiB of HBM per device.

v0:
```python
import math

import jax
import jax.numpy as jnp
from jax import lax
from jax.experimental import pallas as pl
from jax.experimental.pallas import tpu as pltpu
from jax.sharding import PartitionSpec as P


def swap(value, axis, mask):
    pairs = [(source, source ^ mask) for source in range(lax.axis_size(axis))]
    return lax.ppermute(value, axis, pairs)


def pick(blocks, index):
    return lax.dynamic_index_in_dim(blocks, index, 0, keepdims=False)


def scale_kernel(sub, start_ref, gate_ref, up_ref, gate_scale_ref, up_scale_ref, out_ref):
    rows, half_units = gate_ref.shape[1:]
    base = start_ref[0] + pl.program_id(0) * rows
    for value_ref, scale_ref, offset in (
        (gate_ref, gate_scale_ref, 0),
        (up_ref, up_scale_ref, half_units),
    ):
        for piece in range(rows // sub):
            block = (base + piece * sub) // 128
            here = slice(piece * sub, (piece + 1) * sub)
            row = jnp.concatenate(
                [jnp.full((1, 128), scale_ref[block, j]) for j in range(half_units // 128)], 1
            )
            scaled = value_ref[0, here, :].astype(jnp.float32) * row
            out_ref[here, offset : offset + half_units] = scaled.astype(jnp.bfloat16)


def scaled_weights(gate_values, up_values, gate_scales, up_scales, start_row):
    feat_cols, half_units = gate_values.shape[1:]
    sub = math.gcd(feat_cols, 128)
    rows = max(r for r in range(sub, 257, sub) if feat_cols % r == 0)
    value_spec = pl.BlockSpec((1, rows, half_units), lambda i, start: (0, i, 0))
    scale_spec = pl.BlockSpec(memory_space=pltpu.SMEM)
    return pl.pallas_call(
        lambda *refs: scale_kernel(sub, *refs),
        out_shape=jax.ShapeDtypeStruct((feat_cols, 2 * half_units), jnp.bfloat16),
        grid_spec=pltpu.PrefetchScalarGridSpec(
            num_scalar_prefetch=1,
            grid=(feat_cols // rows,),
            in_specs=[value_spec, value_spec, scale_spec, scale_spec],
            out_specs=pl.BlockSpec((rows, 2 * half_units), lambda i, start: (i, 0)),
        ),
        compiler_params=pltpu.CompilerParams(vmem_limit_bytes=24 * 2**20),
        cost_estimate=pl.CostEstimate(
            flops=2 * feat_cols * half_units,
            bytes_accessed=8 * feat_cols * half_units,
            transcendentals=0,
        ),
        name="scale_weights",
    )(start_row[None], gate_values, up_values, gate_scales[0], up_scales[0])


def rows_of(counts_ref, expert):
    first = jnp.int32(0)
    live = jnp.int32(0)
    for other in range(counts_ref.shape[1]):
        count = counts_ref[0, other]
        first = first + jnp.where(other < expert, count, 0)
        live = jnp.where(other == expert, count, live)
    return first, live


def pack_kernel(capacity, chip_ref, counts_ref, tokens_ref, out_ref):
    row_total = tokens_ref.shape[0]
    row = lax.broadcasted_iota(jnp.int32, (capacity, row_total), 1)
    slot = lax.broadcasted_iota(jnp.int32, (capacity, row_total), 0)
    hits = []
    for mask in range(out_ref.shape[0] // capacity):
        first, live = rows_of(counts_ref, chip_ref[0] ^ mask)
        hits.append(((row == first + slot) & (slot < live)).astype(jnp.float32))
    chooser = jnp.concatenate(hits, 0).astype(jnp.bfloat16)
    out_ref[...] = jnp.dot(
        chooser, tokens_ref[...], preferred_element_type=jnp.float32
    ).astype(jnp.bfloat16)


def packed_rows(tokens, counts, chip, capacity):
    row_total, feat_cols = tokens.shape
    experts = counts.shape[1]
    smem = pl.BlockSpec(memory_space=pltpu.SMEM)
    vmem = pl.BlockSpec(memory_space=pltpu.VMEM)
    return pl.pallas_call(
        lambda *refs: pack_kernel(capacity, *refs),
        out_shape=jax.ShapeDtypeStruct((experts * capacity, feat_cols), jnp.bfloat16),
        in_specs=[smem, smem, vmem],
        out_specs=vmem,
        cost_estimate=pl.CostEstimate(
            flops=2 * experts * capacity * row_total * feat_cols,
            bytes_accessed=2 * (row_total + experts * capacity) * feat_cols,
            transcendentals=0,
        ),
        name="pack_rows",
    )(chip[None], counts, tokens)


def combine_kernel(masks, chip_ref, counts_ref, *refs):
    piece_refs, out_ref = refs[:-1], refs[-1]
    capacity = piece_refs[0].shape[0]
    row_total = out_ref.shape[0]
    row = lax.broadcasted_iota(jnp.int32, (row_total, capacity), 0)
    slot = lax.broadcasted_iota(jnp.int32, (row_total, capacity), 1)
    total = None
    for mask, piece_ref in zip(masks, piece_refs):
        first, live = rows_of(counts_ref, chip_ref[0] ^ mask)
        placer = ((row == first + slot) & (slot < live)).astype(jnp.bfloat16)
        term = jnp.dot(placer, piece_ref[...], preferred_element_type=jnp.float32)
        total = term if total is None else total + term
    out_ref[...] = total.astype(jnp.bfloat16)


def combined_rows(pieces, masks, counts, chip, row_total):
    capacity, feat_cols = pieces[0].shape
    smem = pl.BlockSpec(memory_space=pltpu.SMEM)
    vmem = pl.BlockSpec(memory_space=pltpu.VMEM)
    return pl.pallas_call(
        lambda *refs: combine_kernel(masks, *refs),
        out_shape=jax.ShapeDtypeStruct((row_total, feat_cols), jnp.bfloat16),
        in_specs=[smem, smem] + [vmem] * len(pieces),
        out_specs=vmem,
        cost_estimate=pl.CostEstimate(
            flops=2 * len(pieces) * capacity * row_total * feat_cols,
            bytes_accessed=2 * (row_total + len(pieces) * capacity) * feat_cols,
            transcendentals=0,
        ),
        name="combine_rows",
    )(chip[None], counts, *pieces)


def weight_kernel(count, *refs):
    input_refs, grad_refs = refs[:count], refs[count : 2 * count]
    gate_ref, up_ref, held = refs[2 * count :]
    rows = input_refs[0].shape[0]
    half_units = gate_ref.shape[2]

    @pl.when(pl.program_id(0) == 0)
    def _():
        for place, grad_ref in enumerate(grad_refs):
            held[place * rows : (place + 1) * rows, :] = grad_ref[...]

    inputs = jnp.concatenate([input_ref[...] for input_ref in input_refs], 0)
    for out_ref, offset in ((gate_ref, 0), (up_ref, half_units)):
        out_ref[0] = lax.dot_general(
            inputs,
            held[:, offset : offset + half_units],
            (((0,), (0,)), ((), ())),
            preferred_element_type=jnp.float32,
        ).astype(jnp.bfloat16)


def weight_grads(inputs, grads):
    count = len(inputs)
    rows, feat_cols = inputs[0].shape
    units = grads[0].shape[1]
    tile = 256 if feat_cols % 256 == 0 else feat_cols
    out = jax.ShapeDtypeStruct((1, feat_cols, units // 2), jnp.bfloat16)
    out_spec = pl.BlockSpec((1, tile, units // 2), lambda i: (0, i, 0))
    return pl.pallas_call(
        lambda *refs: weight_kernel(count, *refs),
        out_shape=(out, out),
        grid=(feat_cols // tile,),
        in_specs=[pl.BlockSpec((rows, tile), lambda i: (0, i))] * count
        + [pl.BlockSpec((rows, units), lambda i: (0, 0))] * count,
        out_specs=(out_spec, out_spec),
        scratch_shapes=[pltpu.VMEM((count * rows, units), jnp.bfloat16)],
        compiler_params=pltpu.CompilerParams(vmem_limit_bytes=32 * 2**20),
        cost_estimate=pl.CostEstimate(
            flops=2 * count * rows * feat_cols * units,
            bytes_accessed=2 * (count * rows * (feat_cols + units) + feat_cols * units),
            transcendentals=0,
        ),
        name="weight_grads",
    )(*inputs, *grads)


def earlier(value, *needed):
    return lax.optimization_barrier((value,) + needed)[0]


def add_rounded(first, second):
    return (first.astype(jnp.float32) + second.astype(jnp.float32)).astype(jnp.bfloat16)


def towards_middle(size, step):
    return [(step - 1, step), (size - step, size - 1 - step)]


def from_middle(size, step):
    return [(target, source) for source, target in towards_middle(size, size // 2 - step)]


def between_middle(size):
    return [(size // 2 - 1, size // 2), (size // 2, size // 2 - 1)]


def to_middle(size, end):
    return [(end, size // 2 - 1), (size - 1 - end, size // 2)]


def on_device(tokens, counts, gate_values, up_values, gate_scales, up_scales, grad_hidden):
    row_total, feat_cols = tokens.shape
    experts = counts.shape[1]
    capacity = min(4 * row_total // experts, row_total // 2)
    n_expert = lax.axis_size("expert")
    n_fsdp = lax.axis_size("fsdp")
    chips = n_expert // 2
    high_chip = chips // 2
    half_line = n_fsdp // 2
    half_units = gate_values.shape[2]
    parity = lax.axis_index("expert") % 2
    chip = lax.axis_index("expert") // 2
    index = lax.axis_index("fsdp")
    is_low = index < half_line
    keeps_first = is_low == (chip < high_chip)

    packed = packed_rows(tokens, counts, chip, capacity)
    packed = packed.reshape(chips, capacity, feat_cols)
    near = [mask for mask in range(high_chip) if mask % 2 == 0]
    far = [mask for mask in range(high_chip) if mask % 2 == 1]
    near = near + [mask + high_chip for mask in near]
    far = far + [mask + high_chip for mask in far]

    def arrive(masks):
        blocks = [
            swap(packed[mask], "expert", 2 * mask) if mask else packed[mask] for mask in masks
        ]
        return jnp.concatenate(blocks, 0)

    own_near, own_far = arrive(near), arrive(far)

    own_cot = earlier(grad_hidden[0].reshape(2, capacity, half_units), packed)
    cots = [
        lax.ppermute(own_cot, "fsdp", to_middle(n_fsdp, end)) for end in range(half_line - 1)
    ]
    cots = jnp.stack(cots + [own_cot])

    weights = scaled_weights(
        gate_values, up_values, gate_scales, up_scales, index * feat_cols
    )

    groups = [(near, 0), (far, 0), (far, 1), (near, 1)]
    inputs = [own_near, own_far, swap(own_far, "expert", 1), swap(own_near, "expert", 1)]
    inputs[2] = earlier(inputs[2], cots)

    hiddens = jnp.zeros((half_line, 2, capacity, half_units), jnp.bfloat16)
    sums = []
    for order in range(len(groups)):
        running = partial = jnp.dot(
            inputs[order], weights, preferred_element_type=jnp.float32
        ).astype(jnp.bfloat16)
        for step in range(1, half_line):
            if step > 1:
                running = add_rounded(partial, came)
            came = lax.ppermute(running, "fsdp", towards_middle(n_fsdp, step))
        sums.append((partial, came))

    wholes, inner, acts, backs, pieces = [], [], [], [], []
    for order, (masks, side) in enumerate(groups):
        rows = len(masks) * capacity
        which = parity ^ side
        partial, came = sums[order]
        if order >= 1:
            came = earlier(came, acts[order - 1])
        running = add_rounded(partial, came)
        first, second = running[: rows // 2], running[rows // 2 :]
        kept = jnp.where(keeps_first, first, second)
        given = jnp.where(keeps_first, second, first)
        if order >= 2:
            given = earlier(given, inner[order - 2])
        came = lax.ppermute(given, "fsdp", between_middle(n_fsdp))
        pre = kept.astype(jnp.float32) + came.astype(jnp.float32)
        gate_pre = pre[:, :half_units]
        up_pre = pre[:, half_units:]
        owners = [
            chip ^ jnp.where(keeps_first, mask, mask + high_chip)
            for mask in masks[: len(masks) // 2]
        ]
        places = [jnp.where(is_low, owner, n_fsdp - 1 - owner) for owner in owners]
        places = [jnp.clip(place, 0, half_line - 1) for place in places]
        cot = jnp.concatenate([pick(pick(cots, place), which) for place in places], 0)
        cot = cot.astype(jnp.float32)
        sigmoid_gate = jax.nn.sigmoid(gate_pre)
        hidden = (gate_pre * sigmoid_gate * up_pre).astype(jnp.bfloat16)
        grad_gate_pre = cot * up_pre * sigmoid_gate * (1.0 + gate_pre * (1.0 - sigmoid_gate))
        grad_up_pre = cot * gate_pre * sigmoid_gate
        for turn, place in enumerate(places):
            hiddens = lax.dynamic_update_slice(
                hiddens,
                hidden[None, None, turn * capacity : (turn + 1) * capacity],
                (place, which, 0, 0),
            )
        own_grads = jnp.concatenate(
            [grad_gate_pre.astype(jnp.bfloat16), grad_up_pre.astype(jnp.bfloat16)], 1
        )
        acts.append(own_grads)
        if order >= 2:
            own_grads = earlier(own_grads, backs[order - 2])
        came = lax.ppermute(own_grads, "fsdp", between_middle(n_fsdp))
        inner.append(came)
        whole = jnp.where(
            keeps_first,
            jnp.concatenate([own_grads, came], 0),
            jnp.concatenate([came, own_grads], 0),
        )
        for step in range(1, half_line):
            came = lax.ppermute(whole, "fsdp", from_middle(n_fsdp, step))
            here = (index == half_line - 1 - step) | (index == half_line + step)
            whole = jnp.where(here, came, whole)
        wholes.append(whole)
        if order == len(groups) - 1:
            whole, *pieces = lax.optimization_barrier((whole, *pieces))
        back = lax.dot_general(
            whole, weights, (((1,), (1,)), ((), ())), preferred_element_type=jnp.float32
        ).astype(jnp.bfloat16)
        backs.append(back)
        back = back.reshape(len(masks), capacity, feat_cols)
        for turn, mask in enumerate(masks):
            jump = 2 * mask + side
            pieces.append(swap(back[turn], "expert", jump) if jump else back[turn])

    hiddens = earlier(hiddens, wholes[-1])
    hidden = hiddens[half_line - 1]
    for end in range(half_line - 1):
        came = lax.ppermute(
            hiddens[end],
            "fsdp",
            [(target, source) for source, target in to_middle(n_fsdp, end)],
        )
        hidden = jnp.where((index == end) | (index == n_fsdp - 1 - end), came, hidden)
    hidden = hidden.reshape(1, 2 * capacity, half_units)

    grad_gate, grad_up = weight_grads(inputs, wholes)
    grad_tokens = combined_rows(
        pieces, [mask for masks, side in groups for mask in masks], counts, chip, row_total
    )
    return (hidden, grad_gate, grad_up, grad_tokens)


def solution(mesh):
    in_specs = (
        P("expert", "fsdp"),
        P("expert", None),
        P("expert", "fsdp", None),
        P("expert", "fsdp", None),
        P("expert", None, None),
        P("expert", None, None),
        P("expert", "fsdp", None),
    )
    out_specs = (
        P("expert", "fsdp", None),
        P("expert", "fsdp", None),
        P("expert", "fsdp", None),
        P("expert", "fsdp"),
    )
    return jax.shard_map(
        on_device, mesh=mesh, in_specs=in_specs, out_specs=out_specs, check_vma=False
    )
```

profile of v0, /device:TPU:0, one launch (start us, length us, event | category | flops | bytes accessed | tf_op | source)
XLA Modules:
  0.0 142.1 jit_solution(10521136446372348113)
XLA Ops:
  0.6 2.3 %pack_rows.1 = bf16[256,1792]{1,0:T(8,128)(2,1)} custom-call(s32[1]{0:T(128)} %bitcast.refs_0_, s32[1,4]{1,0:T(1,128)} %refs_1_.5, bf16[128,1792]{1,0:T(8,128)(2,1)} %refs_2_.2), custom_call_target="tpu_custom_call" | custom-call | flops 117440512 | bytes 1376256 | tf_op jit(solution)/shard_map/pack_rows/pallas_call | solution.py:91
  3.0 1.3 fusion.28
  4.3 3.0 %collective-permute-start = (bf16[64,1792]{1,0:T(8,128)(2,1)S(1)}, bf16[64,1792]{1,0:T(8,128)(2,1)S(1)}, u32[]{:S(2)}, u32[]{:S(2)}) collective-permute-start(bf16[64,1792]{1,0:T(8,128)(2,1)S(1)} %get-tuple-element.50), channel_id=1, source_target_pairs={{0,16},{4,20},{8,24},{12,28},{16,0},{20,4},{24,8},{28,12},{1,17},{... | collective-permute-start | bytes 688136 | tf_op jit(solution)/shard_map/ppermute | solution.py:13
  7.4 3.5 %collective-permute-start.6 = (bf16[2,64,1024]{2,1,0:T(8,128)(2,1)}, bf16[2,64,1024]{2,1,0:T(8,128)(2,1)S(1)}, u32[]{:S(2)}, u32[]{:S(2)}) collective-permute-start(bf16[2,64,1024]{2,1,0:T(8,128)(2,1)} %bitcast.65), channel_id=1, source_target_pairs={{0,1},{3,2},{4,5},{7,6},{8,9},{11,10},{12,13},{15,14},{16,17},{19,... | collective-permute-start | bytes 786440 | tf_op jit(solution)/shard_map/ppermute | solution.py:241
  10.9 1.5 %collective-permute-start.4 = (bf16[64,1792]{1,0:T(8,128)(2,1)S(1)}, bf16[64,1792]{1,0:T(8,128)(2,1)S(1)}, u32[]{:S(2)}, u32[]{:S(2)}) collective-permute-start(bf16[64,1792]{1,0:T(8,128)(2,1)S(1)} %get-tuple-element.48), channel_id=1, source_target_pairs={{0,24},{4,28},{8,16},{12,20},{16,8},{20,12},{24,0},{28,4},{1,25},{... | collective-permute-start | bytes 688136 | tf_op jit(solution)/shard_map/ppermute | solution.py:13
  14.4 2.0 %copy-done = bf16[1,1792,1024]{2,1,0:T(8,128)(2,1)S(1)} copy-done((bf16[1,1792,1024]{2,1,0:T(8,128)(2,1)S(1)}, bf16[1,1792,1024]{2,1,0:T(8,128)(2,1)}, u32[]{:S(2)}) %copy-start) | copy-done | bytes 3670040
  16.5 2.0 %copy-done.1 = bf16[1,1792,1024]{2,1,0:T(8,128)(2,1)S(1)} copy-done((bf16[1,1792,1024]{2,1,0:T(8,128)(2,1)S(1)}, bf16[1,1792,1024]{2,1,0:T(8,128)(2,1)}, u32[]{:S(2)}) %copy-start.1) | copy-done | bytes 3670040
  18.5 3.0 %scale_weights.1 = bf16[1792,2048]{1,0:T(8,128)(2,1)S(1)} custom-call(s32[1]{0:T(128)} %bitcast.1.refs_0_, bf16[1,1792,1024]{2,1,0:T(8,128)(2,1)S(1)} %copy-done, bf16[1,1792,1024]{2,1,0:T(8,128)(2,1)S(1)} %copy-done.1, f32[56,8]{1,0:T(8,128)S(1)} %bitcast.63, f32[56,8]{1,0:T(8,128)S(1)} %bitcast.64), custom_call_target="tpu_custom_call" | custom-call | flops 3670016 | bytes 14680064 | tf_op jit(solution)/shard_map/scale_weights/pallas_call | solution.py:43
  22.7 1.3 collective-permute-start.1
  25.8 1.3 collective-permute-start.5
  27.2 9.2 %collective-permute-done.1 = bf16[128,2048]{1,0:T(8,128)(2,1)S(1)} collective-permute-done((bf16[128,2048]{1,0:T(8,128)(2,1)S(1)}, bf16[128,2048]{1,0:T(8,128)(2,1)S(1)}, u32[]{:S(2)}, u32[]{:S(2)}) %collective-permute-start.1) | collective-permute-done | bytes 524320 | tf_op jit(solution)/shard_map/ppermute | solution.py:262
  38.5 7.2 %collective-permute-start.9 = (bf16[128,2048]{1,0:T(8,128)(2,1)S(1)}, bf16[128,2048]{1,0:T(8,128)(2,1)S(1)}, u32[]{:S(2)}, u32[]{:S(2)}) collective-permute-start(bf16[128,2048]{1,0:T(8,128)(2,1)S(1)} %convolution_convert_fusion.5), channel_id=1, source_target_pairs={{0,1},{3,2},{4,5},{7,6},{8,9},{11,10},{12,13},{15,14},{16,17},{19,... | collective-permute-start | bytes 1572872 | tf_op jit(solution)/shard_map/ppermute | solution.py:262
  46.0 1.5 %collective-permute-done.5 = bf16[128,2048]{1,0:T(8,128)(2,1)S(1)} collective-permute-done((bf16[128,2048]{1,0:T(8,128)(2,1)S(1)}, bf16[128,2048]{1,0:T(8,128)(2,1)S(1)}, u32[]{:S(2)}, u32[]{:S(2)}) %collective-permute-start.5) | collective-permute-done | bytes 524320 | tf_op jit(solution)/shard_map/ppermute | solution.py:262
  49.6 7.2 %collective-permute-start.13 = (bf16[128,2048]{1,0:T(8,128)(2,1)S(1)}, bf16[128,2048]{1,0:T(8,128)(2,1)S(1)}, u32[]{:S(2)}, u32[]{:S(2)}) collective-permute-start(bf16[128,2048]{1,0:T(8,128)(2,1)S(1)} %convolution_convert_fusion.4), channel_id=1, source_target_pairs={{0,1},{3,2},{4,5},{7,6},{8,9},{11,10},{12,13},{15,14},{16,17},{19,... | collective-permute-start | bytes 1572872 | tf_op jit(solution)/shard_map/ppermute | solution.py:262
  59.8 1.3 collective-permute-start.20
  61.5 8.4 %collective-permute-done.13 = bf16[128,2048]{1,0:T(8,128)(2,1)S(1)} collective-permute-done((bf16[128,2048]{1,0:T(8,128)(2,1)S(1)}, bf16[128,2048]{1,0:T(8,128)(2,1)S(1)}, u32[]{:S(2)}, u32[]{:S(2)}) %collective-permute-start.13) | collective-permute-done | bytes 524320 | tf_op jit(solution)/shard_map/ppermute | solution.py:262
  70.8 1.3 collective-permute-start.16
  72.2 9.2 %collective-permute-done.20 = bf16[128,2048]{1,0:T(8,128)(2,1)S(1)} collective-permute-done((bf16[128,2048]{1,0:T(8,128)(2,1)S(1)}, bf16[128,2048]{1,0:T(8,128)(2,1)S(1)}, u32[]{:S(2)}, u32[]{:S(2)}) %collective-permute-start.20) | collective-permute-done | bytes 524320 | tf_op jit(solution)/shard_map/ppermute | solution.py:314
  81.5 2.5 %convolution_convert_fusion.2 = bf16[128,1792]{1,0:T(8,128)(2,1)S(1)} fusion(bf16[128,2048]{1,0:T(8,128)(2,1)S(1)} %broadcast_select_fusion.1.refs_4_, bf16[1792,2048]{1,0:T(8,128)(2,1)S(1)} %scale_weights.1), kind=kOutput, calls=%fused_computation.2 | convolution fusion | flops 939753472 | bytes 8323072 | tf_op jit(solution)/shard_map/dot_general | solution.py:320
  85.7 1.6 %collective-permute-start.23 = (bf16[64,1792]{1,0:T(8,128)(2,1)S(1)}, bf16[64,1792]{1,0:T(8,128)(2,1)S(1)}, u32[]{:S(2)}, u32[]{:S(2)}) collective-permute-start(bf16[64,1792]{1,0:T(8,128)(2,1)S(1)} %get-tuple-element.58), channel_id=1, source_target_pairs={{0,16},{4,20},{8,24},{12,28},{16,0},{20,4},{24,8},{28,12},{1,17},{... | collective-permute-start | bytes 688136 | tf_op jit(solution)/shard_map/ppermute | solution.py:13
  87.5 1.5 %collective-permute-start.22 = (bf16[128,2048]{1,0:T(8,128)(2,1)S(1)}, bf16[128,2048]{1,0:T(8,128)(2,1)S(1)}, u32[]{:S(2)}, u32[]{:S(2)}) collective-permute-start(bf16[128,2048]{1,0:T(8,128)(2,1)S(1)} %maximum_select_fusion.3), channel_id=1, source_target_pairs={{1,0},{2,3},{5,4},{6,7},{9,8},{10,11},{13,12},{14,15},{17,16},{18,... | collective-permute-start | bytes 1572872 | tf_op jit(solution)/shard_map/ppermute | solution.py:314
  89.0 4.0 %collective-permute-done.16 = bf16[128,2048]{1,0:T(8,128)(2,1)S(1)} collective-permute-done((bf16[128,2048]{1,0:T(8,128)(2,1)S(1)}, bf16[128,2048]{1,0:T(8,128)(2,1)S(1)}, u32[]{:S(2)}, u32[]{:S(2)}) %collective-permute-start.16) | collective-permute-done | bytes 524320 | tf_op jit(solution)/shard_map/ppermute | solution.py:314
  93.0 2.5 %convolution_convert_fusion.3 = bf16[128,1792]{1,0:T(8,128)(2,1)S(1)} fusion(bf16[128,2048]{1,0:T(8,128)(2,1)S(1)} %broadcast_select_fusion.3.refs_5_, bf16[1792,2048]{1,0:T(8,128)(2,1)S(1)} %scale_weights.1), kind=kOutput, calls=%fused_computation.3 | convolution fusion | flops 939753472 | bytes 8323072 | tf_op jit(solution)/shard_map/dot_general | solution.py:320
  96.3 2.5 %collective-permute-start.25 = (bf16[64,1792]{1,0:T(8,128)(2,1)S(1)}, bf16[64,1792]{1,0:T(8,128)(2,1)S(1)}, u32[]{:S(2)}, u32[]{:S(2)}) collective-permute-start(bf16[64,1792]{1,0:T(8,128)(2,1)S(1)} %get-tuple-element.56), channel_id=1, source_target_pairs={{0,24},{4,28},{8,16},{12,20},{16,8},{20,12},{24,0},{28,4},{1,25},{... | collective-permute-start | bytes 688136 | tf_op jit(solution)/shard_map/ppermute | solution.py:13
  100.8 4.5 %collective-permute-done.22 = bf16[128,2048]{1,0:T(8,128)(2,1)S(1)} collective-permute-done((bf16[128,2048]{1,0:T(8,128)(2,1)S(1)}, bf16[128,2048]{1,0:T(8,128)(2,1)S(1)}, u32[]{:S(2)}, u32[]{:S(2)}) %collective-permute-start.22) | collective-permute-done | bytes 524320 | tf_op jit(solution)/shard_map/ppermute | solution.py:314
  105.3 2.5 %convolution_convert_fusion.1 = bf16[128,1792]{1,0:T(8,128)(2,1)S(1)} fusion(bf16[128,2048]{1,0:T(8,128)(2,1)S(1)} %broadcast_select_fusion.refs_6_, bf16[1792,2048]{1,0:T(8,128)(2,1)S(1)} %scale_weights.1), kind=kOutput, calls=%fused_computation.1 | convolution fusion | flops 939753472 | bytes 8323072 | tf_op jit(solution)/shard_map/dot_general | solution.py:320
  107.9 8.6 %collective-permute-done.18 = bf16[128,2048]{1,0:T(8,128)(2,1)S(1)} collective-permute-done((bf16[128,2048]{1,0:T(8,128)(2,1)S(1)}, bf16[128,2048]{1,0:T(8,128)(2,1)S(1)}, u32[]{:S(2)}, u32[]{:S(2)}) %collective-permute-start.18) | collective-permute-done | bytes 524320 | tf_op jit(solution)/shard_map/ppermute | solution.py:314
  116.7 7.7 %collective-permute-done.26.refs_6_ = bf16[64,1792]{1,0:T(8,128)(2,1)S(1)} collective-permute-done((bf16[64,1792]{1,0:T(8,128)(2,1)S(1)}, bf16[64,1792]{1,0:T(8,128)(2,1)S(1)}, u32[]{:S(2)}, u32[]{:S(2)}) %collective-permute-start.26) | collective-permute-done | bytes 229408 | tf_op jit(solution)/shard_map/ppermute | solution.py:13
  124.4 2.5 %convolution_convert_fusion = bf16[128,1792]{1,0:T(8,128)(2,1)S(1)} fusion(bf16[128,2048]{1,0:T(8,128)(2,1)S(1)} %broadcast_select_fusion.2.refs_7_, bf16[1792,2048]{1,0:T(8,128)(2,1)S(1)} %scale_weights.1), kind=kOutput, calls=%fused_computation | convolution fusion | flops 939753472 | bytes 8323072 | tf_op jit(solution)/shard_map/dot_general | solution.py:320
  127.0 1.3 collective-permute-start.29
  130.1 6.5 %weight_grads.1 = (bf16[1,1792,1024]{2,1,0:T(8,128)(2,1)}, bf16[1,1792,1024]{2,1,0:T(8,128)(2,1)}) custom-call(bf16[128,1792]{1,0:T(8,128)(2,1)S(1)} %pad_maximum_fusion.1.refs_0_, bf16[128,1792]{1,0:T(8,128)(2,1)S(1)} %constant_dynamic-update-slice_fusion.refs_1_, bf16[128,1792]{1,0:T(8,128)(2,1)S(1)} %collective-permute-done.8.refs_2_, ...), custom_call_target="tpu_custom_call" | custom-call | flops 3758096384 | bytes 11272192 | tf_op jit(solution)/shard_map/weight_grads/pallas_call | solution.py:166
  138.0 3.4 %combine_rows.1 = bf16[128,1792]{1,0:T(8,128)(2,1)} custom-call(s32[1]{0:T(128)} %bitcast.refs_0_, s32[1,4]{1,0:T(1,128)} %refs_1_.5, bf16[64,1792]{1,0:T(8,128)(2,1)} %get-tuple-element.33.refs_2_, bf16[64,1792]{1,0:T(8,128)(2,1)} %copy-done.3, bf16[64,1792]{1,0:T(8,128)(2,1)} %copy-done.5, bf16[64,1792]{1,0:T(8,128)(2,1)} %copy-done.4, ...), custom_call_target="tpu_custom_call" | custom-call | flops 234881024 | bytes 2293760 | tf_op jit(solution)/shard_map/combine_rows/pallas_call | solution.py:124
  (105 shorter events, 22.3 us)
Async XLA Ops:
  4.3 17.1 %collective-permute-start = (bf16[64,1792]{1,0:T(8,128)(2,1)S(1)}, bf16[64,1792]{1,0:T(8,128)(2,1)S(1)}, u32[]{:S(2)}, u32[]{:S(2)}) collective-permute-start(bf16[64,1792]{1,0:T(8,128)(2,1)S(1)} %get-tuple-element.50), channel_id=1, source_target_pairs={{0,16},{4,20},{8,24},{12,28},{16,0},{20,4},{24,8},{28,12},{1,17},{... | collective-permute-start | bytes 688136 | tf_op jit(solution)/shard_map/ppermute | solution.py:13
  7.4 38.4 %collective-permute-start.6 = (bf16[2,64,1024]{2,1,0:T(8,128)(2,1)}, bf16[2,64,1024]{2,1,0:T(8,128)(2,1)S(1)}, u32[]{:S(2)}, u32[]{:S(2)}) collective-permute-start(bf16[2,64,1024]{2,1,0:T(8,128)(2,1)} %bitcast.65), channel_id=1, source_target_pairs={{0,1},{3,2},{4,5},{7,6},{8,9},{11,10},{12,13},{15,14},{16,17},{19,... | collective-permute-start | bytes 786440 | tf_op jit(solution)/shard_map/ppermute | solution.py:241
  10.9 13.2 %collective-permute-start.4 = (bf16[64,1792]{1,0:T(8,128)(2,1)S(1)}, bf16[64,1792]{1,0:T(8,128)(2,1)S(1)}, u32[]{:S(2)}, u32[]{:S(2)}) collective-permute-start(bf16[64,1792]{1,0:T(8,128)(2,1)S(1)} %get-tuple-element.48), channel_id=1, source_target_pairs={{0,24},{4,28},{8,16},{12,20},{16,8},{20,12},{24,0},{28,4},{1,25},{... | collective-permute-start | bytes 688136 | tf_op jit(solution)/shard_map/ppermute | solution.py:13
  12.4 11.7 %collective-permute-start.3 = (bf16[64,1792]{1,0:T(8,128)(2,1)S(1)}, bf16[64,1792]{1,0:T(8,128)(2,1)S(1)}, u32[]{:S(2)}, u32[]{:S(2)}) collective-permute-start(bf16[64,1792]{1,0:T(8,128)(2,1)S(1)} %get-tuple-element.49), channel_id=1, source_target_pairs={{0,8},{4,12},{8,0},{12,4},{16,24},{20,28},{24,16},{28,20},{1,9},{5... | collective-permute-start | bytes 688136 | tf_op jit(solution)/shard_map/ppermute | solution.py:13
  21.5 26.9 %collective-permute-start.12 = (bf16[128,1792]{1,0:T(8,128)(2,1)S(1)}, bf16[128,1792]{1,0:T(8,128)(2,1)S(1)}, u32[]{:S(2)}, u32[]{:S(2)}) collective-permute-start(bf16[128,1792]{1,0:T(8,128)(2,1)S(1)} %pad_maximum_fusion.1.refs_0_), channel_id=1, source_target_pairs={{0,4},{4,0},{8,12},{12,8},{16,20},{20,16},{24,28},{28,24},{1,5},{5... | collective-permute-start | bytes 1376264 | tf_op jit(solution)/shard_map/ppermute | solution.py:13
  22.7 13.6 %collective-permute-start.1 = (bf16[128,2048]{1,0:T(8,128)(2,1)S(1)}, bf16[128,2048]{1,0:T(8,128)(2,1)S(1)}, u32[]{:S(2)}, u32[]{:S(2)}) collective-permute-start(bf16[128,2048]{1,0:T(8,128)(2,1)S(1)} %convolution_convert_fusion.7), channel_id=1, source_target_pairs={{0,1},{3,2},{4,5},{7,6},{8,9},{11,10},{12,13},{15,14},{16,17},{19,... | collective-permute-start | bytes 1572872 | tf_op jit(solution)/shard_map/ppermute | solution.py:262
  24.1 3.0 %collective-permute-start.8 = (bf16[128,1792]{1,0:T(8,128)(2,1)S(1)}, bf16[128,1792]{1,0:T(8,128)(2,1)S(1)}, u32[]{:S(2)}, u32[]{:S(2)}) collective-permute-start(bf16[128,1792]{1,0:T(8,128)(2,1)S(1)} %constant_dynamic-update-slice_fusion.refs_1_), channel_id=1, source_target_pairs={{0,4},{4,0},{8,12},{12,8},{16,20},{20,16},{24,28},{28,24},{1,5},{5... | collective-permute-start | bytes 1376264 | tf_op jit(solution)/shard_map/ppermute | solution.py:13
  25.8 21.7 %collective-permute-start.5 = (bf16[128,2048]{1,0:T(8,128)(2,1)S(1)}, bf16[128,2048]{1,0:T(8,128)(2,1)S(1)}, u32[]{:S(2)}, u32[]{:S(2)}) collective-permute-start(bf16[128,2048]{1,0:T(8,128)(2,1)S(1)} %convolution_convert_fusion.6), channel_id=1, source_target_pairs={{0,1},{3,2},{4,5},{7,6},{8,9},{11,10},{12,13},{15,14},{16,17},{19,... | collective-permute-start | bytes 1572872 | tf_op jit(solution)/shard_map/ppermute | solution.py:262
  36.5 9.2 %collective-permute-start.2 = (bf16[64,2048]{1,0:T(8,128)(2,1)S(1)}, bf16[64,2048]{1,0:T(8,128)(2,1)S(1)}, u32[]{:S(2)}, u32[]{:S(2)}) collective-permute-start(bf16[64,2048]{1,0:T(8,128)(2,1)S(1)} %broadcast_select_fusion.7), channel_id=1, source_target_pairs={{1,2},{2,1},{5,6},{6,5},{9,10},{10,9},{13,14},{14,13},{17,18},{18,... | collective-permute-start | bytes 786440 | tf_op jit(solution)/shard_map/ppermute | solution.py:278
  38.5 20.3 %collective-permute-start.9 = (bf16[128,2048]{1,0:T(8,128)(2,1)S(1)}, bf16[128,2048]{1,0:T(8,128)(2,1)S(1)}, u32[]{:S(2)}, u32[]{:S(2)}) collective-permute-start(bf16[128,2048]{1,0:T(8,128)(2,1)S(1)} %convolution_convert_fusion.5), channel_id=1, source_target_pairs={{0,1},{3,2},{4,5},{7,6},{8,9},{11,10},{12,13},{15,14},{16,17},{19,... | collective-permute-start | bytes 1572872 | tf_op jit(solution)/shard_map/ppermute | solution.py:262
  47.7 9.9 %collective-permute-start.7 = (bf16[64,2048]{1,0:T(8,128)(2,1)S(1)}, bf16[64,2048]{1,0:T(8,128)(2,1)S(1)}, u32[]{:S(2)}, u32[]{:S(2)}) collective-permute-start(bf16[64,2048]{1,0:T(8,128)(2,1)S(1)} %broadcast_select_fusion.6), channel_id=1, source_target_pairs={{1,2},{2,1},{5,6},{6,5},{9,10},{10,9},{13,14},{14,13},{17,18},{18,... | collective-permute-start | bytes 786440 | tf_op jit(solution)/shard_map/ppermute | solution.py:278
  49.6 20.3 %collective-permute-start.13 = (bf16[128,2048]{1,0:T(8,128)(2,1)S(1)}, bf16[128,2048]{1,0:T(8,128)(2,1)S(1)}, u32[]{:S(2)}, u32[]{:S(2)}) collective-permute-start(bf16[128,2048]{1,0:T(8,128)(2,1)S(1)} %convolution_convert_fusion.4), channel_id=1, source_target_pairs={{0,1},{3,2},{4,5},{7,6},{8,9},{11,10},{12,13},{15,14},{16,17},{19,... | collective-permute-start | bytes 1572872 | tf_op jit(solution)/shard_map/ppermute | solution.py:262
  56.8 2.2 %collective-permute-start.10 = (bf16[64,2048]{1,0:T(8,128)(2,1)S(1)}, bf16[64,2048]{1,0:T(8,128)(2,1)S(1)}, u32[]{:S(2)}, u32[]{:S(2)}) collective-permute-start(bf16[64,2048]{1,0:T(8,128)(2,1)S(1)} %pad_maximum_fusion.2), channel_id=1, source_target_pairs={{1,2},{2,1},{5,6},{6,5},{9,10},{10,9},{13,14},{14,13},{17,18},{18,... | collective-permute-start | bytes 786440 | tf_op jit(solution)/shard_map/ppermute | solution.py:306
  57.9 12.1 %collective-permute-start.14 = (bf16[64,2048]{1,0:T(8,128)(2,1)S(1)}, bf16[64,2048]{1,0:T(8,128)(2,1)S(1)}, u32[]{:S(2)}, u32[]{:S(2)}) collective-permute-start(bf16[64,2048]{1,0:T(8,128)(2,1)S(1)} %pad_maximum_fusion.3), channel_id=1, source_target_pairs={{1,2},{2,1},{5,6},{6,5},{9,10},{10,9},{13,14},{14,13},{17,18},{18,... | collective-permute-start | bytes 786440 | tf_op jit(solution)/shard_map/ppermute | solution.py:306
  59.0 2.2 %collective-permute-start.11 = (bf16[64,2048]{1,0:T(8,128)(2,1)S(1)}, bf16[64,2048]{1,0:T(8,128)(2,1)S(1)}, u32[]{:S(2)}, u32[]{:S(2)}) collective-permute-start(bf16[64,2048]{1,0:T(8,128)(2,1)S(1)} %broadcast_select_fusion.5), channel_id=1, source_target_pairs={{1,2},{2,1},{5,6},{6,5},{9,10},{10,9},{13,14},{14,13},{17,18},{18,... | collective-permute-start | bytes 786440 | tf_op jit(solution)/shard_map/ppermute | solution.py:278
  59.8 21.7 %collective-permute-start.20 = (bf16[128,2048]{1,0:T(8,128)(2,1)S(1)}, bf16[128,2048]{1,0:T(8,128)(2,1)S(1)}, u32[]{:S(2)}, u32[]{:S(2)}) collective-permute-start(bf16[128,2048]{1,0:T(8,128)(2,1)S(1)} %maximum_select_fusion.2), channel_id=1, source_target_pairs={{1,0},{2,3},{5,4},{6,7},{9,8},{10,11},{13,12},{14,15},{17,16},{18,... | collective-permute-start | bytes 1572872 | tf_op jit(solution)/shard_map/ppermute | solution.py:314
  70.0 14.7 %collective-permute-start.15 = (bf16[64,2048]{1,0:T(8,128)(2,1)S(1)}, bf16[64,2048]{1,0:T(8,128)(2,1)S(1)}, u32[]{:S(2)}, u32[]{:S(2)}) collective-permute-start(bf16[64,2048]{1,0:T(8,128)(2,1)S(1)} %broadcast_select_fusion.4), channel_id=1, source_target_pairs={{1,2},{2,1},{5,6},{6,5},{9,10},{10,9},{13,14},{14,13},{17,18},{18,... | collective-permute-start | bytes 786440 | tf_op jit(solution)/shard_map/ppermute | solution.py:278
  70.8 22.1 %collective-permute-start.16 = (bf16[128,2048]{1,0:T(8,128)(2,1)S(1)}, bf16[128,2048]{1,0:T(8,128)(2,1)S(1)}, u32[]{:S(2)}, u32[]{:S(2)}) collective-permute-start(bf16[128,2048]{1,0:T(8,128)(2,1)S(1)} %maximum_select_fusion), channel_id=1, source_target_pairs={{1,0},{2,3},{5,4},{6,7},{9,8},{10,11},{13,12},{14,15},{17,16},{18,... | collective-permute-start | bytes 1572872 | tf_op jit(solution)/shard_map/ppermute | solution.py:314
  85.0 2.4 %collective-permute-start.21 = (bf16[64,2048]{1,0:T(8,128)(2,1)S(1)}, bf16[64,2048]{1,0:T(8,128)(2,1)S(1)}, u32[]{:S(2)}, u32[]{:S(2)}) collective-permute-start(bf16[64,2048]{1,0:T(8,128)(2,1)S(1)} %pad_maximum_fusion.4), channel_id=1, source_target_pairs={{1,2},{2,1},{5,6},{6,5},{9,10},{10,9},{13,14},{14,13},{17,18},{18,... | collective-permute-start | bytes 786440 | tf_op jit(solution)/shard_map/ppermute | solution.py:306
  85.7 30.9 %collective-permute-start.23 = (bf16[64,1792]{1,0:T(8,128)(2,1)S(1)}, bf16[64,1792]{1,0:T(8,128)(2,1)S(1)}, u32[]{:S(2)}, u32[]{:S(2)}) collective-permute-start(bf16[64,1792]{1,0:T(8,128)(2,1)S(1)} %get-tuple-element.58), channel_id=1, source_target_pairs={{0,16},{4,20},{8,24},{12,28},{16,0},{20,4},{24,8},{28,12},{1,17},{... | collective-permute-start | bytes 688136 | tf_op jit(solution)/shard_map/ppermute | solution.py:13
  87.5 17.7 %collective-permute-start.22 = (bf16[128,2048]{1,0:T(8,128)(2,1)S(1)}, bf16[128,2048]{1,0:T(8,128)(2,1)S(1)}, u32[]{:S(2)}, u32[]{:S(2)}) collective-permute-start(bf16[128,2048]{1,0:T(8,128)(2,1)S(1)} %maximum_select_fusion.3), channel_id=1, source_target_pairs={{1,0},{2,3},{5,4},{6,7},{9,8},{10,11},{13,12},{14,15},{17,16},{18,... | collective-permute-start | bytes 1572872 | tf_op jit(solution)/shard_map/ppermute | solution.py:314
  95.6 3.8 %collective-permute-start.17 = (bf16[64,2048]{1,0:T(8,128)(2,1)S(1)}, bf16[64,2048]{1,0:T(8,128)(2,1)S(1)}, u32[]{:S(2)}, u32[]{:S(2)}) collective-permute-start(bf16[64,2048]{1,0:T(8,128)(2,1)S(1)} %pad_maximum_fusion.5), channel_id=1, source_target_pairs={{1,2},{2,1},{5,6},{6,5},{9,10},{10,9},{13,14},{14,13},{17,18},{18,... | collective-permute-start | bytes 786440 | tf_op jit(solution)/shard_map/ppermute | solution.py:306
  96.3 20.4 %collective-permute-start.25 = (bf16[64,1792]{1,0:T(8,128)(2,1)S(1)}, bf16[64,1792]{1,0:T(8,128)(2,1)S(1)}, u32[]{:S(2)}, u32[]{:S(2)}) collective-permute-start(bf16[64,1792]{1,0:T(8,128)(2,1)S(1)} %get-tuple-element.56), channel_id=1, source_target_pairs={{0,24},{4,28},{8,16},{12,20},{16,8},{20,12},{24,0},{28,4},{1,25},{... | collective-permute-start | bytes 688136 | tf_op jit(solution)/shard_map/ppermute | solution.py:13
  98.8 17.9 %collective-permute-start.24 = (bf16[64,1792]{1,0:T(8,128)(2,1)S(1)}, bf16[64,1792]{1,0:T(8,128)(2,1)S(1)}, u32[]{:S(2)}, u32[]{:S(2)}) collective-permute-start(bf16[64,1792]{1,0:T(8,128)(2,1)S(1)} %get-tuple-element.57), channel_id=1, source_target_pairs={{0,8},{4,12},{8,0},{12,4},{16,24},{20,28},{24,16},{28,20},{1,9},{5... | collective-permute-start | bytes 688136 | tf_op jit(solution)/shard_map/ppermute | solution.py:13
  99.5 17.1 %collective-permute-start.18 = (bf16[128,2048]{1,0:T(8,128)(2,1)S(1)}, bf16[128,2048]{1,0:T(8,128)(2,1)S(1)}, u32[]{:S(2)}, u32[]{:S(2)}) collective-permute-start(bf16[128,2048]{1,0:T(8,128)(2,1)S(1)} %maximum_select_fusion.1), channel_id=1, source_target_pairs={{1,0},{2,3},{5,4},{6,7},{9,8},{10,11},{13,12},{14,15},{17,16},{18,... | collective-permute-start | bytes 1572872 | tf_op jit(solution)/shard_map/ppermute | solution.py:314
  107.9 8.8 %collective-permute-start.27 = (bf16[64,1792]{1,0:T(8,128)(2,1)S(1)}, bf16[64,1792]{1,0:T(8,128)(2,1)S(1)}, u32[]{:S(2)}, u32[]{:S(2)}) collective-permute-start(bf16[64,1792]{1,0:T(8,128)(2,1)S(1)} %get-tuple-element.54), channel_id=1, source_target_pairs={{0,28},{4,24},{8,20},{12,16},{16,12},{20,8},{24,4},{28,0},{1,29},{... | collective-permute-start | bytes 688136 | tf_op jit(solution)/shard_map/ppermute | solution.py:13
  116.6 7.9 %collective-permute-start.26 = (bf16[64,1792]{1,0:T(8,128)(2,1)S(1)}, bf16[64,1792]{1,0:T(8,128)(2,1)S(1)}, u32[]{:S(2)}, u32[]{:S(2)}) collective-permute-start(bf16[64,1792]{1,0:T(8,128)(2,1)S(1)} %get-tuple-element.55), channel_id=1, source_target_pairs={{0,12},{4,8},{8,4},{12,0},{16,28},{20,24},{24,20},{28,16},{1,13},{... | collective-permute-start | bytes 688136 | tf_op jit(solution)/shard_map/ppermute | solution.py:13
  116.7 19.9 %copy-start.3 = (bf16[64,1792]{1,0:T(8,128)(2,1)}, bf16[64,1792]{1,0:T(8,128)(2,1)S(1)}, u32[]{:S(2)}) copy-start(bf16[64,1792]{1,0:T(8,128)(2,1)S(1)} %collective-permute-done.23.refs_3_) | copy-start | bytes 688132
  116.7 19.9 %copy-start.4 = (bf16[64,1792]{1,0:T(8,128)(2,1)}, bf16[64,1792]{1,0:T(8,128)(2,1)S(1)}, u32[]{:S(2)}) copy-start(bf16[64,1792]{1,0:T(8,128)(2,1)S(1)} %collective-permute-done.25.refs_5_) | copy-start | bytes 688132
  127.0 9.5 %collective-permute-start.29 = (bf16[64,1792]{1,0:T(8,128)(2,1)S(1)}, bf16[64,1792]{1,0:T(8,128)(2,1)S(1)}, u32[]{:S(2)}, u32[]{:S(2)}) collective-permute-start(bf16[64,1792]{1,0:T(8,128)(2,1)S(1)} %get-tuple-element.52), channel_id=1, source_target_pairs={{0,20},{4,16},{8,28},{12,24},{16,4},{20,0},{24,12},{28,8},{1,21},{... | collective-permute-start | bytes 688136 | tf_op jit(solution)/shard_map/ppermute | solution.py:13
  128.3 8.2 %collective-permute-start.28 = (bf16[64,1792]{1,0:T(8,128)(2,1)S(1)}, bf16[64,1792]{1,0:T(8,128)(2,1)S(1)}, u32[]{:S(2)}, u32[]{:S(2)}) collective-permute-start(bf16[64,1792]{1,0:T(8,128)(2,1)S(1)} %get-tuple-element.53), channel_id=1, source_target_pairs={{0,4},{4,0},{8,12},{12,8},{16,20},{20,16},{24,28},{28,24},{1,5},{5... | collective-permute-start | bytes 688136 | tf_op jit(solution)/shard_map/ppermute | solution.py:13
  128.8 12.6 %collective-permute-start.19 = (bf16[2,64,1024]{2,1,0:T(8,128)(2,1)S(1)}, bf16[2,64,1024]{2,1,0:T(8,128)(2,1)S(1)}, u32[]{:S(2)}, u32[]{:S(2)}) collective-permute-start(bf16[2,64,1024]{2,1,0:T(8,128)(2,1)S(1)} %slice_bitcast_fusion), channel_id=1, source_target_pairs={{1,0},{2,3},{5,4},{6,7},{9,8},{10,11},{13,12},{14,15},{17,16},{18,... | collective-permute-start | bytes 786440 | tf_op jit(solution)/shard_map/ppermute | solution.py:332
  (8 other events, 66.5 us)
where the time goes:
time: 143 us; the launch traced here: 142 us
  waiting for transfers between devices  53.3 us (37%)
  starting transfers between devices  44.9 us (31%)
  Pallas kernels  15.2 us (11%)
  matrix products  14.6 us (10%)
  local copies, waits for them, and re-layouts  9.26 us (6%)
  other arithmetic  3.46 us (2%)
    ppermute x4, waiting for transfers between devices, on_device(): came = lax.ppermute(whole, 'fsdp', from_middle(n_fsdp, step))  26.3 us
    ppermute x4, waiting for transfers between devices, on_device(): came = lax.ppermute(running, 'fsdp', towards_middle(n_fsdp, step))  19.2 us
    ppermute x4, starting transfers between devices, on_device(): came = lax.ppermute(running, 'fsdp', towards_middle(n_fsdp, step))  17.1 us
    ppermute x12, starting transfers between devices, swap(): return lax.ppermute(value, axis, pairs)  12.1 us
    dot_general x4, matrix products, on_device(): lax.dot_general(whole, weights, (((1,), (1,)), ((), ())), preferred_eleme...  10.1 us
    ppermute x12, waiting for transfers between devices, swap(): return lax.ppermute(value, axis, pairs)  7.74 us
    unnamed x23, local copies, waits for them, and re-layouts  7.02 us
    pallas_call x1, Pallas kernels, weight_grads(): pl.pallas_call(lambda *refs: weight_kernel(count, *refs), out_shape=(out,...  6.46 us
  transfers between devices with their start and end apart: 30, of which 9 were waited for; matrix products, arithmetic and copies ran while one was open for 12% of the time, Pallas kernels for 9%

commit v1 on v0

v1 whole, which is shorter than its diff:
```python
import math

import jax
import jax.numpy as jnp
from jax import lax
from jax.experimental import pallas as pl
from jax.experimental.pallas import tpu as pltpu
from jax.sharding import PartitionSpec as P


def swap(value, axis, mask):
    pairs = [(source, source ^ mask) for source in range(lax.axis_size(axis))]
    return lax.ppermute(value, axis, pairs)


def pick(blocks, index):
    return lax.dynamic_index_in_dim(blocks, index, 0, keepdims=False)


def scale_kernel(
    sub, start_ref, gate_ref, up_ref, gate_scale_ref, up_scale_ref, out_ref, gate_rows, up_rows
):
    rows, half_units = gate_ref.shape[1:]
    base = start_ref[0] + pl.program_id(0) * rows

    @pl.when(pl.program_id(0) == 0)
    def _():
        for scale_ref, grown in ((gate_scale_ref, gate_rows), (up_scale_ref, up_rows)):
            for j in range(half_units // 128):
                grown[:, j * 128 : (j + 1) * 128] = jnp.broadcast_to(
                    scale_ref[0, :, j : j + 1], (grown.shape[0], 128)
                )

    for value_ref, grown, offset in ((gate_ref, gate_rows, 0), (up_ref, up_rows, half_units)):
        for piece in range(rows // sub):
            block = (base + piece * sub) // 128
            here = slice(piece * sub, (piece + 1) * sub)
            scaled = value_ref[0, here, :].astype(jnp.float32) * grown[pl.ds(block, 1), :]
            out_ref[here, offset : offset + half_units] = scaled.astype(jnp.bfloat16)


def scaled_weights(gate_values, up_values, gate_scales, up_scales, start_row):
    feat_cols, half_units = gate_values.shape[1:]
    sub = math.gcd(feat_cols, 128)
    rows = max(r for r in range(sub, 257, sub) if feat_cols % r == 0)
    value_spec = pl.BlockSpec((1, rows, half_units), lambda i, start: (0, i, 0))
    scale_spec = pl.BlockSpec(gate_scales.shape, lambda i, start: (0, 0, 0))
    grown = pltpu.VMEM((gate_scales.shape[1], half_units), jnp.float32)
    return pl.pallas_call(
        lambda *refs: scale_kernel(sub, *refs),
        out_shape=jax.ShapeDtypeStruct((feat_cols, 2 * half_units), jnp.bfloat16),
        grid_spec=pltpu.PrefetchScalarGridSpec(
            num_scalar_prefetch=1,
            grid=(feat_cols // rows,),
            in_specs=[value_spec, value_spec, scale_spec, scale_spec],
            out_specs=pl.BlockSpec((rows, 2 * half_units), lambda i, start: (i, 0)),
            scratch_shapes=[grown, grown],
        ),
        compiler_params=pltpu.CompilerParams(vmem_limit_bytes=24 * 2**20),
        cost_estimate=pl.CostEstimate(
            flops=2 * feat_cols * half_units,
            bytes_accessed=8 * feat_cols * half_units,
            transcendentals=0,
        ),
        name="scale_weights",
    )(
        start_row[None],
        pltpu.with_memory_space_constraint(gate_values, pltpu.HBM),
        pltpu.with_memory_space_constraint(up_values, pltpu.HBM),
        gate_scales,
        up_scales,
    )


def rows_of(counts_ref, expert):
    first = jnp.int32(0)
    live = jnp.int32(0)
    for other in range(counts_ref.shape[1]):
        count = counts_ref[0, other]
        first = first + jnp.where(other < expert, count, 0)
        live = jnp.where(other == expert, count, live)
    return first, live


def pack_kernel(chip_ref, counts_ref, tokens_ref, *out_refs):
    row_total = tokens_ref.shape[0]
    capacity = out_refs[0].shape[0]
    row = lax.broadcasted_iota(jnp.int32, (capacity, row_total), 1)
    slot = lax.broadcasted_iota(jnp.int32, (capacity, row_total), 0)
    hits = []
    for mask in range(len(out_refs)):
        first, live = rows_of(counts_ref, chip_ref[0] ^ mask)
        hits.append(((row == first + slot) & (slot < live)).astype(jnp.float32))
    chooser = jnp.concatenate(hits, 0).astype(jnp.bfloat16)
    chosen = jnp.dot(chooser, tokens_ref[...], preferred_element_type=jnp.float32)
    for mask, out_ref in enumerate(out_refs):
        out_ref[...] = chosen[mask * capacity : (mask + 1) * capacity].astype(jnp.bfloat16)


def packed_rows(tokens, counts, chip, capacity):
    row_total, feat_cols = tokens.shape
    experts = counts.shape[1]
    smem = pl.BlockSpec(memory_space=pltpu.SMEM)
    vmem = pl.BlockSpec(memory_space=pltpu.VMEM)
    block = jax.ShapeDtypeStruct((capacity, feat_cols), jnp.bfloat16)
    return pl.pallas_call(
        pack_kernel,
        out_shape=(block,) * experts,
        in_specs=[smem, smem, vmem],
        out_specs=(vmem,) * experts,
        cost_estimate=pl.CostEstimate(
            flops=2 * experts * capacity * row_total * feat_cols,
            bytes_accessed=2 * (row_total + experts * capacity) * feat_cols,
            transcendentals=0,
        ),
        name="pack_rows",
    )(chip[None], counts, tokens)


def combine_kernel(masks, chip_ref, counts_ref, *refs):
    piece_refs, out_ref = refs[:-1], refs[-1]
    capacity = piece_refs[0].shape[0]
    row_total = out_ref.shape[0]
    row = lax.broadcasted_iota(jnp.int32, (capacity, row_total), 1)
    slot = lax.broadcasted_iota(jnp.int32, (capacity, row_total), 0)
    hits = []
    for mask in masks:
        first, live = rows_of(counts_ref, chip_ref[0] ^ mask)
        hits.append(((row == first + slot) & (slot < live)).astype(jnp.float32))
    out_ref[...] = lax.dot_general(
        jnp.concatenate(hits, 0).astype(jnp.bfloat16),
        jnp.concatenate([piece_ref[...] for piece_ref in piece_refs], 0),
        (((0,), (0,)), ((), ())),
        preferred_element_type=jnp.float32,
    ).astype(jnp.bfloat16)


def combined_rows(pieces, masks, counts, chip, row_total):
    capacity, feat_cols = pieces[0].shape
    smem = pl.BlockSpec(memory_space=pltpu.SMEM)
    vmem = pl.BlockSpec(memory_space=pltpu.VMEM)
    return pl.pallas_call(
        lambda *refs: combine_kernel(masks, *refs),
        out_shape=jax.ShapeDtypeStruct((row_total, feat_cols), jnp.bfloat16),
        in_specs=[smem, smem] + [vmem] * len(pieces),
        out_specs=vmem,
        cost_estimate=pl.CostEstimate(
            flops=2 * len(pieces) * capacity * row_total * feat_cols,
            bytes_accessed=2 * (row_total + len(pieces) * capacity) * feat_cols,
            transcendentals=0,
        ),
        name="combine_rows",
    )(chip[None], counts, *pieces)


def weight_kernel(count, *refs):
    input_refs, grad_refs = refs[:count], refs[count : 2 * count]
    gate_ref, up_ref, held = refs[2 * count :]
    half_units = gate_ref.shape[2]

    @pl.when(pl.program_id(0) == 0)
    def _():
        place = 0
        for grad_ref in grad_refs:
            held[place : place + grad_ref.shape[0], :] = grad_ref[...]
            place += grad_ref.shape[0]

    inputs = jnp.concatenate([input_ref[...] for input_ref in input_refs], 0)
    for out_ref, offset in ((gate_ref, 0), (up_ref, half_units)):
        out_ref[0] = lax.dot_general(
            inputs,
            held[:, offset : offset + half_units],
            (((0,), (0,)), ((), ())),
            preferred_element_type=jnp.float32,
        ).astype(jnp.bfloat16)


def weight_grads(inputs, grads):
    count = len(inputs)
    rows = sum(value.shape[0] for value in inputs)
    feat_cols = inputs[0].shape[1]
    units = grads[0].shape[1]
    tile = 256 if feat_cols % 256 == 0 else feat_cols
    out = jax.ShapeDtypeStruct((1, feat_cols, units // 2), jnp.bfloat16)
    out_spec = pl.BlockSpec((1, tile, units // 2), lambda i: (0, i, 0))
    return pl.pallas_call(
        lambda *refs: weight_kernel(count, *refs),
        out_shape=(out, out),
        grid=(feat_cols // tile,),
        in_specs=[pl.BlockSpec((value.shape[0], tile), lambda i: (0, i)) for value in inputs]
        + [pl.BlockSpec(value.shape, lambda i: (0, 0)) for value in grads],
        out_specs=(out_spec, out_spec),
        scratch_shapes=[pltpu.VMEM((rows, units), jnp.bfloat16)],
        compiler_params=pltpu.CompilerParams(vmem_limit_bytes=32 * 2**20),
        cost_estimate=pl.CostEstimate(
            flops=2 * rows * feat_cols * units,
            bytes_accessed=2 * (rows * (feat_cols + units) + feat_cols * units),
            transcendentals=0,
        ),
        name="weight_grads",
    )(*inputs, *grads)


def earlier(value, *needed):
    return lax.optimization_barrier((value,) + needed)[0]


def add_rounded(first, second):
    return (first.astype(jnp.float32) + second.astype(jnp.float32)).astype(jnp.bfloat16)


def towards_middle(size, step):
    return [(step - 1, step), (size - step, size - 1 - step)]


def from_middle(size, step):
    return [(target, source) for source, target in towards_middle(size, size // 2 - step)]


def between_middle(size):
    low = size // 2 - 1
    swapped = {low: low + 1, low + 1: low}
    return [(source, swapped.get(source, source)) for source in range(size)]


def to_middle(size, end):
    return [(end, size // 2 - 1), (size - 1 - end, size // 2)]


def on_device(tokens, counts, gate_values, up_values, gate_scales, up_scales, grad_hidden):
    row_total, feat_cols = tokens.shape
    experts = counts.shape[1]
    capacity = min(4 * row_total // experts, row_total // 2)
    n_expert = lax.axis_size("expert")
    n_fsdp = lax.axis_size("fsdp")
    chips = n_expert // 2
    high_chip = chips // 2
    half_line = n_fsdp // 2
    half_units = gate_values.shape[2]
    parity = lax.axis_index("expert") % 2
    chip = lax.axis_index("expert") // 2
    index = lax.axis_index("fsdp")
    is_low = index < half_line
    keeps_first = is_low == (chip < high_chip)

    packed = packed_rows(tokens, counts, chip, capacity)
    near = [mask for mask in range(chips) if mask % 2 == 0]
    far = [mask for mask in range(chips) if mask % 2 == 1]
    blocks = {}
    for mask in near + far:
        blocks[mask, 0] = swap(packed[mask], "expert", 2 * mask) if mask else packed[mask]
    for masks in (far, near):
        there = swap(jnp.concatenate([blocks[mask, 0] for mask in masks], 0), "expert", 1)
        for turn, mask in enumerate(masks):
            blocks[mask, 1] = there[turn * capacity : (turn + 1) * capacity]

    part = capacity // 2
    own_cot = earlier(grad_hidden[0].reshape(2, 2, part, half_units), packed[0])
    cots = [
        lax.ppermute(own_cot, "fsdp", to_middle(n_fsdp, end)) for end in range(half_line - 1)
    ]
    cots = jnp.stack(cots + [own_cot])

    weights = scaled_weights(
        gate_values, up_values, gate_scales, up_scales, index * feat_cols
    )

    units = [
        (mask, side, half)
        for masks, side in ((near, 0), (far, 0), (far, 1), (near, 1))
        for mask in masks
        if mask < high_chip
        for half in range(2)
    ]
    step = len(units) // 8
    bounds = [0, step, 3 * step, 5 * step, 7 * step, 8 * step]
    groups = [units[low:high] for low, high in zip(bounds[:-1], bounds[1:])]

    def blocks_of(group):
        return [unit for unit in group] + [
            (mask + high_chip, side, half) for mask, side, half in group
        ]

    inputs = []
    for group in groups:
        inputs.append(
            jnp.concatenate(
                [
                    blocks[mask, side][half * part : (half + 1) * part]
                    for mask, side, half in blocks_of(group)
                ],
                0,
            )
        )

    hiddens = jnp.zeros((half_line, 2, 2, part, half_units), jnp.bfloat16)
    wholes, inner, acts, backs, pieces, back_parts = [], [], [], [], {}, {}
    sums = None
    for order, group in enumerate(groups):
        if order == 0:
            partials = []
            for place in range(len(groups)):
                values = inputs[place]
                if place == 2:
                    values = earlier(values, cots)
                partials.append(
                    jnp.dot(values, weights, preferred_element_type=jnp.float32).astype(
                        jnp.bfloat16
                    )
                )
        partial = partials[order]
        running = partial if sums is None else earlier(partial, sums)
        for hop in range(1, half_line):
            if hop > 1:
                running = add_rounded(running_base, came)
            running_base = partial
            came = lax.ppermute(running, "fsdp", towards_middle(n_fsdp, hop))
        if order >= 1:
            came = earlier(came, acts[order - 1])
        sums = add_rounded(partial, came)
        rows = sums.shape[0]
        first, second = sums[: rows // 2], sums[rows // 2 :]
        kept = jnp.where(keeps_first, first, second)
        given = jnp.where(keeps_first, second, first)
        if order >= 2:
            given = earlier(given, inner[order - 2])
        came = lax.ppermute(given, "fsdp", between_middle(n_fsdp))
        if order >= 2:
            came = earlier(came, backs[order - 2])
        pre = kept.astype(jnp.float32) + came.astype(jnp.float32)
        gate_pre = pre[:, :half_units]
        up_pre = pre[:, half_units:]
        spots = []
        for mask, side, half in group:
            owner = chip ^ jnp.where(keeps_first, mask, mask + high_chip)
            place = jnp.where(is_low, owner, n_fsdp - 1 - owner)
            spots.append((jnp.clip(place, 0, half_line - 1), parity ^ side, half))
        cot = jnp.concatenate(
            [
                lax.dynamic_slice(
                    cots, (*spot, 0, 0), (1, 1, 1, part, half_units)
                ).reshape(part, half_units)
                for spot in spots
            ],
            0,
        ).astype(jnp.float32)
        sigmoid_gate = jax.nn.sigmoid(gate_pre)
        hidden = (gate_pre * sigmoid_gate * up_pre).astype(jnp.bfloat16)
        grad_gate_pre = cot * up_pre * sigmoid_gate * (1.0 + gate_pre * (1.0 - sigmoid_gate))
        grad_up_pre = cot * gate_pre * sigmoid_gate
        for turn, spot in enumerate(spots):
            hiddens = lax.dynamic_update_slice(
                hiddens,
                hidden[None, None, None, turn * part : (turn + 1) * part],
                (*spot, 0, 0),
            )
        own_grads = jnp.concatenate(
            [grad_gate_pre.astype(jnp.bfloat16), grad_up_pre.astype(jnp.bfloat16)], 1
        )
        acts.append(own_grads)
        came = lax.ppermute(own_grads, "fsdp", between_middle(n_fsdp))
        inner.append(came)
        whole = jnp.where(
            keeps_first,
            jnp.concatenate([own_grads, came], 0),
            jnp.concatenate([came, own_grads], 0),
        )
        for hop in range(1, half_line):
            came = lax.ppermute(whole, "fsdp", from_middle(n_fsdp, hop))
            if order >= 1 and hop == half_line - 1:
                came = earlier(came, backs[order - 1])
                early = [key for key in pieces if key not in fresh]
                came, *held = lax.optimization_barrier((came, *(pieces[key] for key in early)))
                pieces.update(zip(early, held))
            here = (index == half_line - 1 - hop) | (index == half_line + hop)
            whole = jnp.where(here, came, whole)
        wholes.append(whole)
        back = lax.dot_general(
            whole, weights, (((1,), (1,)), ((), ())), preferred_element_type=jnp.float32
        ).astype(jnp.bfloat16)
        backs.append(back)
        fresh = []
        for turn, (mask, side, half) in enumerate(blocks_of(group)):
            back_parts[mask, side, half] = back[turn * part : (turn + 1) * part]
            if half == 1:
                block = jnp.concatenate(
                    [back_parts[mask, side, 0], back_parts[mask, side, 1]], 0
                )
                jump = 2 * mask + side
                pieces[mask, side] = swap(block, "expert", jump) if jump else block
                fresh.append((mask, side))

    hiddens = earlier(hiddens, wholes[-1])
    hidden = hiddens[half_line - 1]
    for end in range(half_line - 1):
        came = lax.ppermute(
            hiddens[end],
            "fsdp",
            [(target, source) for source, target in to_middle(n_fsdp, end)],
        )
        hidden = jnp.where((index == end) | (index == n_fsdp - 1 - end), came, hidden)
    hidden = hidden.reshape(1, 2 * capacity, half_units)

    grad_gate, grad_up = weight_grads(inputs, wholes)
    masks = [mask for mask, side in pieces]
    grad_tokens = combined_rows(list(pieces.values()), masks, counts, chip, row_total)
    return (hidden, grad_gate, grad_up, grad_tokens)


def solution(mesh):
    in_specs = (
        P("expert", "fsdp"),
        P("expert", None),
        P("expert", "fsdp", None),
        P("expert", "fsdp", None),
        P("expert", None, None),
        P("expert", None, None),
        P("expert", "fsdp", None),
    )
    out_specs = (
        P("expert", "fsdp", None),
        P("expert", "fsdp", None),
        P("expert", "fsdp", None),
        P("expert", "fsdp"),
    )
    return jax.shard_map(
        on_device, mesh=mesh, in_specs=in_specs, out_specs=out_specs, check_vma=False
    )
```

time: 143 us -> 153 us (1.070)
  starting transfers between devices: 44.9 us -> 59.6 us
  local copies, waits for them, and re-layouts: 9.26 us -> 2.67 us
  waiting for transfers between devices: 53.3 us -> 47.6 us
  matrix products: 14.6 us -> 18.4 us
  Pallas kernels: 15.2 us -> 17.5 us
    ppermute x8 -> x10, starting transfers between devices: 22.4 us -> 35.7 us  [the longest x5 29 us: on_device(): came = lax.ppermute(running, 'fsdp', towards_middle(n_fsdp, hop))]
    unnamed x23 -> x20, local copies, waits for them, and re-layouts: 7.02 us -> 2.26 us
    ppermute x8 -> x10, waiting for transfers between devices: 45.5 us -> 41.9 us  [the longest x5 27.8 us: on_device(): came = lax.ppermute(whole, 'fsdp', from_middle(n_fsdp, hop))]
    pallas_call x1, Pallas kernels: 2.96 us -> 5.92 us  [scaled_weights(): pl.pallas_call(lambda *refs: scale_kernel(sub, *refs), out_shape=jax.Shap...]
    dot_general x4 -> x5, matrix products: 10.1 us -> 12.3 us  [on_device(): lax.dot_general(whole, weights, (((1,), (1,)), ((), ())), preferred_eleme...]
    ppermute x12, waiting for transfers between devices: 7.74 us -> 5.67 us  [swap(): return lax.ppermute(value, axis, pairs)]
    slice x5 -> x10, local copies, waits for them, and re-layouts: 2.15 us -> 0.27 us  [the longest x6 0.13 us: on_device(): blocks[mask, side][half * part:(half + 1) * part]]
    dot_general x4 -> x5, matrix products: 4.49 us -> 6.14 us  [on_device(): jnp.dot(values, weights, preferred_element_type=jnp.float32)]
  transfers between devices with their start and end apart: 30 -> 34, of which waited for: 9 -> 10; matrix products, arithmetic and copies ran while one was open for 12% -> 14% of each run, Pallas kernels for 9% -> 10%
where the time goes in v1:
time: 153 us; the launch traced here: 152 us
  starting transfers between devices  59.6 us (39%)
  waiting for transfers between devices  47.6 us (31%)
  matrix products  18.4 us (12%)
  Pallas kernels  17.5 us (11%)
  other arithmetic  4.43 us (3%)
  local copies, waits for them, and re-layouts  2.67 us (2%)
  between operations  1.7 us (1%)
    ppermute x5, starting transfers between devices, on_device(): came = lax.ppermute(running, 'fsdp', towards_middle(n_fsdp, hop))  29 us
    ppermute x5, waiting for transfers between devices, on_device(): came = lax.ppermute(whole, 'fsdp', from_middle(n_fsdp, hop))  27.8 us
    ppermute x5, waiting for transfers between devices, on_device(): came = lax.ppermute(running, 'fsdp', towards_middle(n_fsdp, hop))  14.1 us
    dot_general x5, matrix products, on_device(): lax.dot_general(whole, weights, (((1,), (1,)), ((), ())), preferred_eleme...  12.3 us
    ppermute x12, starting transfers between devices, swap(): return lax.ppermute(value, axis, pairs)  11.9 us
    ppermute x5, starting transfers between devices, on_device(): came = lax.ppermute(whole, 'fsdp', from_middle(n_fsdp, hop))  6.64 us
    pallas_call x1, Pallas kernels, weight_grads(): pl.pallas_call(lambda *refs: weight_kernel(count, *refs), out_shape=(out,...  6.48 us
    dot_general x5, matrix products, on_device(): jnp.dot(values, weights, preferred_element_type=jnp.float32)  6.14 us
  transfers between devices with their start and end apart: 34, of which 10 were waited for; matrix products, arithmetic and copies ran while one was open for 14% of the time, Pallas kernels for 10%

profile of v1, /device:TPU:0, one launch (start us, length us, event | category | flops | bytes accessed | tf_op | source)
XLA Modules:
  0.0 151.9 jit_solution(14621894702304437516)
XLA Ops:
  0.6 2.3 %pack_rows.1 = (bf16[64,1792]{1,0:T(8,128)(2,1)}, bf16[64,1792]{1,0:T(8,128)(2,1)}, bf16[64,1792]{1,0:T(8,128)(2,1)}, bf16[64,1792]{1,0:T(8,128)(2,1)}) custom-call(s32[1]{0:T(128)} %bitcast.chip_ref.refs_0_, s32[1,4]{1,0:T(1,128)} %refs_1_.3, bf16[128,1792]{1,0:T(8,128)(2,1)} %tokens_ref.1), custom_call_target="tpu_custom_call" | custom-call | flops 117440512 | bytes 1376256 | tf_op jit(solution)/shard_map/pack_rows/pallas_call | solution.py:106
  2.9 3.0 %collective-permute-start = (bf16[64,1792]{1,0:T(8,128)(2,1)}, bf16[64,1792]{1,0:T(8,128)(2,1)S(1)}, u32[]{:S(2)}, u32[]{:S(2)}) collective-permute-start(bf16[64,1792]{1,0:T(8,128)(2,1)} %get-tuple-element.40), channel_id=1, source_target_pairs={{0,16},{4,20},{8,24},{12,28},{16,0},{20,4},{24,8},{28,12},{1,17},{... | collective-permute-start | bytes 688136 | tf_op jit(solution)/shard_map/ppermute | solution.py:13
  5.9 1.5 collective-permute-start.3
  7.4 4.0 %collective-permute-start.6 = (bf16[2,2,32,1024]{3,2,1,0:T(8,128)(2,1)}, bf16[2,2,32,1024]{3,2,1,0:T(8,128)(2,1)S(1)}, u32[]{:S(2)}, u32[]{:S(2)}) collective-permute-start(bf16[2,2,32,1024]{3,2,1,0:T(8,128)(2,1)} %bitcast.74), channel_id=1, source_target_pairs={{0,1},{3,2},{4,5},{7,6},{8,9},{11,10},{12,13},{15,14},{16,17},{19,... | collective-permute-start | bytes 786440 | tf_op jit(solution)/shard_map/ppermute | solution.py:260
  13.0 5.9 %scale_weights.1 = bf16[1792,2048]{1,0:T(8,128)(2,1)S(1)} custom-call(s32[1]{0:T(128)} %bitcast.1.refs_0_, bf16[1,1792,1024]{2,1,0:T(8,128)(2,1)} %refs_1_.2, bf16[1,1792,1024]{2,1,0:T(8,128)(2,1)} %refs_2_.1, f32[1,56,8]{2,1,0:T(8,128)S(1)} %copy.11.refs_3_, f32[1,56,8]{2,1,0:T(8,128)S(1)} %copy.12.refs_4_), custom_call_target="tpu_custom_call" | custom-call | flops 3670016 | bytes 14680064 | tf_op jit(solution)/shard_map/scale_weights/pallas_call | solution.py:49
  19.1 1.4 convolution_convert_fusion.9
  20.5 2.6 %collective-permute-start.1 = (bf16[64,2048]{1,0:T(8,128)(2,1)S(1)}, bf16[64,2048]{1,0:T(8,128)(2,1)S(1)}, u32[]{:S(2)}, u32[]{:S(2)}) collective-permute-start(bf16[64,2048]{1,0:T(8,128)(2,1)S(1)} %convolution_convert_fusion.9), channel_id=1, source_target_pairs={{0,1},{3,2},{4,5},{7,6},{8,9},{11,10},{12,13},{15,14},{16,17},{19,... | collective-permute-start | bytes 786440 | tf_op jit(solution)/shard_map/ppermute | solution.py:317
  24.3 4.9 %collective-permute-done.1 = bf16[64,2048]{1,0:T(8,128)(2,1)S(1)} collective-permute-done((bf16[64,2048]{1,0:T(8,128)(2,1)S(1)}, bf16[64,2048]{1,0:T(8,128)(2,1)S(1)}, u32[]{:S(2)}, u32[]{:S(2)}) %collective-permute-start.1) | collective-permute-done | bytes 262176 | tf_op jit(solution)/shard_map/ppermute | solution.py:317
  30.4 7.2 %collective-permute-start.5 = (bf16[128,2048]{1,0:T(8,128)(2,1)S(1)}, bf16[128,2048]{1,0:T(8,128)(2,1)S(1)}, u32[]{:S(2)}, u32[]{:S(2)}) collective-permute-start(bf16[128,2048]{1,0:T(8,128)(2,1)S(1)} %convolution_convert_fusion.5), channel_id=1, source_target_pairs={{0,1},{3,2},{4,5},{7,6},{8,9},{11,10},{12,13},{15,14},{16,17},{19,... | collective-permute-start | bytes 1572872 | tf_op jit(solution)/shard_map/ppermute | solution.py:317
  41.0 1.4 convolution_convert_fusion.7
  42.5 1.3 collective-permute-start.12
  43.8 9.0 %collective-permute-done.12 = bf16[64,2048]{1,0:T(8,128)(2,1)S(1)} collective-permute-done((bf16[64,2048]{1,0:T(8,128)(2,1)S(1)}, bf16[64,2048]{1,0:T(8,128)(2,1)S(1)}, u32[]{:S(2)}, u32[]{:S(2)}) %collective-permute-start.12) | collective-permute-done | bytes 262176 | tf_op jit(solution)/shard_map/ppermute | solution.py:369
  52.8 2.3 %convolution_convert_fusion.8 = bf16[64,1792]{1,0:T(8,128)(2,1)S(1)} fusion(bf16[64,2048]{1,0:T(8,128)(2,1)S(1)} %broadcast_select_fusion.4.refs_5_, bf16[1792,2048]{1,0:T(8,128)(2,1)S(1)} %scale_weights.1), kind=kOutput, calls=%fused_computation.8 | convolution fusion | flops 469876736 | bytes 7831552 | tf_op jit(solution)/shard_map/dot_general | solution.py:378
  56.0 3.2 %collective-permute-start.9 = (bf16[128,2048]{1,0:T(8,128)(2,1)S(1)}, bf16[128,2048]{1,0:T(8,128)(2,1)S(1)}, u32[]{:S(2)}, u32[]{:S(2)}) collective-permute-start(bf16[128,2048]{1,0:T(8,128)(2,1)S(1)} %convolution_convert_fusion.4), channel_id=1, source_target_pairs={{0,1},{3,2},{4,5},{7,6},{8,9},{11,10},{12,13},{15,14},{16,17},{19,... | collective-permute-start | bytes 1572872 | tf_op jit(solution)/shard_map/ppermute | solution.py:317
  60.2 7.7 %collective-permute-done.9 = bf16[128,2048]{1,0:T(8,128)(2,1)S(1)} collective-permute-done((bf16[128,2048]{1,0:T(8,128)(2,1)S(1)}, bf16[128,2048]{1,0:T(8,128)(2,1)S(1)}, u32[]{:S(2)}, u32[]{:S(2)}) %collective-permute-start.9) | collective-permute-done | bytes 524320 | tf_op jit(solution)/shard_map/ppermute | solution.py:317
  70.2 7.4 %collective-permute-start.14 = (bf16[128,2048]{1,0:T(8,128)(2,1)S(1)}, bf16[128,2048]{1,0:T(8,128)(2,1)S(1)}, u32[]{:S(2)}, u32[]{:S(2)}) collective-permute-start(bf16[128,2048]{1,0:T(8,128)(2,1)S(1)} %convolution_convert_fusion.3), channel_id=1, source_target_pairs={{0,1},{3,2},{4,5},{7,6},{8,9},{11,10},{12,13},{15,14},{16,17},{19,... | collective-permute-start | bytes 1572872 | tf_op jit(solution)/shard_map/ppermute | solution.py:317
  78.8 1.5 collective-permute-start.21
  80.3 3.9 %collective-permute-done.17 = bf16[128,2048]{1,0:T(8,128)(2,1)S(1)} collective-permute-done((bf16[128,2048]{1,0:T(8,128)(2,1)S(1)}, bf16[128,2048]{1,0:T(8,128)(2,1)S(1)}, u32[]{:S(2)}, u32[]{:S(2)}) %collective-permute-start.17) | collective-permute-done | bytes 524320 | tf_op jit(solution)/shard_map/ppermute | solution.py:369
  86.2 8.6 %collective-permute-start.18 = (bf16[64,2048]{1,0:T(8,128)(2,1)S(1)}, bf16[64,2048]{1,0:T(8,128)(2,1)S(1)}, u32[]{:S(2)}, u32[]{:S(2)}) collective-permute-start(bf16[64,2048]{1,0:T(8,128)(2,1)S(1)} %convolution_convert_fusion.7), channel_id=1, source_target_pairs={{0,1},{3,2},{4,5},{7,6},{8,9},{11,10},{12,13},{15,14},{16,17},{19,... | collective-permute-start | bytes 786440 | tf_op jit(solution)/shard_map/ppermute | solution.py:317
  94.9 2.5 %convolution_convert_fusion.2 = bf16[128,1792]{1,0:T(8,128)(2,1)S(1)} fusion(bf16[128,2048]{1,0:T(8,128)(2,1)S(1)} %broadcast_select_fusion.2.refs_6_, bf16[1792,2048]{1,0:T(8,128)(2,1)S(1)} %scale_weights.1), kind=kOutput, calls=%fused_computation.2 | convolution fusion | flops 939753472 | bytes 8323072 | tf_op jit(solution)/shard_map/dot_general | solution.py:378
  99.6 2.5 %convolution_convert_fusion.1 = bf16[128,1792]{1,0:T(8,128)(2,1)S(1)} fusion(bf16[128,2048]{1,0:T(8,128)(2,1)S(1)} %broadcast_select_fusion.1.refs_7_, bf16[1792,2048]{1,0:T(8,128)(2,1)S(1)} %scale_weights.1), kind=kOutput, calls=%fused_computation.1 | convolution fusion | flops 939753472 | bytes 8323072 | tf_op jit(solution)/shard_map/dot_general | solution.py:378
  104.5 1.5 %collective-permute-start.27 = (bf16[64,1792]{1,0:T(8,128)(2,1)S(1)}, bf16[64,1792]{1,0:T(8,128)(2,1)S(1)}, u32[]{:S(2)}, u32[]{:S(2)}) collective-permute-start(bf16[64,1792]{1,0:T(8,128)(2,1)S(1)} %pad_maximum_fusion.13), channel_id=1, source_target_pairs={{0,8},{4,12},{8,0},{12,4},{16,24},{20,28},{24,16},{28,20},{1,9},{5... | collective-permute-start | bytes 688136 | tf_op jit(solution)/shard_map/ppermute | solution.py:13
  106.1 1.6 %collective-permute-start.28 = (bf16[64,1792]{1,0:T(8,128)(2,1)S(1)}, bf16[64,1792]{1,0:T(8,128)(2,1)S(1)}, u32[]{:S(2)}, u32[]{:S(2)}) collective-permute-start(bf16[64,1792]{1,0:T(8,128)(2,1)S(1)} %pad_maximum_fusion.14), channel_id=1, source_target_pairs={{0,24},{4,28},{8,16},{12,20},{16,8},{20,12},{24,0},{28,4},{1,25},{... | collective-permute-start | bytes 688136 | tf_op jit(solution)/shard_map/ppermute | solution.py:13
  110.4 12.7 %collective-permute-done.25 = bf16[128,2048]{1,0:T(8,128)(2,1)S(1)} collective-permute-done((bf16[128,2048]{1,0:T(8,128)(2,1)S(1)}, bf16[128,2048]{1,0:T(8,128)(2,1)S(1)}, u32[]{:S(2)}, u32[]{:S(2)}) %collective-permute-start.25) | collective-permute-done | bytes 524320 | tf_op jit(solution)/shard_map/ppermute | solution.py:369
  123.1 2.5 %convolution_convert_fusion = bf16[128,1792]{1,0:T(8,128)(2,1)S(1)} fusion(bf16[128,2048]{1,0:T(8,128)(2,1)S(1)} %broadcast_select_fusion.refs_8_, bf16[1792,2048]{1,0:T(8,128)(2,1)S(1)} %scale_weights.1), kind=kOutput, calls=%fused_computation | convolution fusion | flops 939753472 | bytes 8323072 | tf_op jit(solution)/shard_map/dot_general | solution.py:378
  125.7 2.4 %collective-permute-done.23 = bf16[64,2048]{1,0:T(8,128)(2,1)S(1)} collective-permute-done((bf16[64,2048]{1,0:T(8,128)(2,1)S(1)}, bf16[64,2048]{1,0:T(8,128)(2,1)S(1)}, u32[]{:S(2)}, u32[]{:S(2)}) %collective-permute-start.23) | collective-permute-done | bytes 262176 | tf_op jit(solution)/shard_map/ppermute | solution.py:369
  128.1 2.3 %convolution_convert_fusion.6 = bf16[64,1792]{1,0:T(8,128)(2,1)S(1)} fusion(bf16[64,2048]{1,0:T(8,128)(2,1)S(1)} %broadcast_select_fusion.3.refs_9_, bf16[1792,2048]{1,0:T(8,128)(2,1)S(1)} %scale_weights.1), kind=kOutput, calls=%fused_computation.6 | convolution fusion | flops 469876736 | bytes 7831552 | tf_op jit(solution)/shard_map/dot_general | solution.py:378
  131.9 3.4 %collective-permute-start.31 = (bf16[64,1792]{1,0:T(8,128)(2,1)S(1)}, bf16[64,1792]{1,0:T(8,128)(2,1)S(1)}, u32[]{:S(2)}, u32[]{:S(2)}) collective-permute-start(bf16[64,1792]{1,0:T(8,128)(2,1)S(1)} %pad_maximum_fusion.16), channel_id=1, source_target_pairs={{0,28},{4,24},{8,20},{12,16},{16,12},{20,8},{24,4},{28,0},{1,29},{... | collective-permute-start | bytes 688136 | tf_op jit(solution)/shard_map/ppermute | solution.py:13
  135.5 6.5 %weight_grads.1 = (bf16[1,1792,1024]{2,1,0:T(8,128)(2,1)}, bf16[1,1792,1024]{2,1,0:T(8,128)(2,1)}) custom-call(bf16[64,1792]{1,0:T(8,128)(2,1)S(1)} %pad_maximum_fusion.9.refs_0_, bf16[128,1792]{1,0:T(8,128)(2,1)S(1)} %pad_maximum_fusion.1.refs_1_, bf16[128,1792]{1,0:T(8,128)(2,1)S(1)} %pad_maximum_fusion.3.refs_2_, ...), custom_call_target="tpu_custom_call" | custom-call | flops 3758096384 | bytes 11272192 | tf_op jit(solution)/shard_map/weight_grads/pallas_call | solution.py:186
  142.0 4.3 %collective-permute-done.31.refs_7_ = bf16[64,1792]{1,0:T(8,128)(2,1)S(1)} collective-permute-done((bf16[64,1792]{1,0:T(8,128)(2,1)S(1)}, bf16[64,1792]{1,0:T(8,128)(2,1)S(1)}, u32[]{:S(2)}, u32[]{:S(2)}) %collective-permute-start.31) | collective-permute-done | bytes 229408 | tf_op jit(solution)/shard_map/ppermute | solution.py:13
  146.3 1.3 collective-permute-done.33.refs_9_
  148.4 2.8 %combine_rows.1 = bf16[128,1792]{1,0:T(8,128)(2,1)} custom-call(s32[1]{0:T(128)} %bitcast.chip_ref.refs_0_, s32[1,4]{1,0:T(1,128)} %refs_1_.3, bf16[64,1792]{1,0:T(8,128)(2,1)} %pad_maximum_fusion.11.refs_2_, bf16[64,1792]{1,0:T(8,128)(2,1)} %copy-done.4, bf16[64,1792]{1,0:T(8,128)(2,1)} %copy-done.2, bf16[64,1792]{1,0:T(8,128)(2,1)} %copy-done.3, ...), custom_call_target="tpu_custom_call" | custom-call | flops 234881024 | bytes 2293760 | tf_op jit(solution)/shard_map/combine_rows/pallas_call | solution.py:142
  (142 shorter events, 24.9 us)
Async XLA Ops:
  2.9 16.1 %collective-permute-start = (bf16[64,1792]{1,0:T(8,128)(2,1)}, bf16[64,1792]{1,0:T(8,128)(2,1)S(1)}, u32[]{:S(2)}, u32[]{:S(2)}) collective-permute-start(bf16[64,1792]{1,0:T(8,128)(2,1)} %get-tuple-element.40), channel_id=1, source_target_pairs={{0,16},{4,20},{8,24},{12,28},{16,0},{20,4},{24,8},{28,12},{1,17},{... | collective-permute-start | bytes 688136 | tf_op jit(solution)/shard_map/ppermute | solution.py:13
  5.9 13.0 %collective-permute-start.3 = (bf16[64,1792]{1,0:T(8,128)(2,1)}, bf16[64,1792]{1,0:T(8,128)(2,1)S(1)}, u32[]{:S(2)}, u32[]{:S(2)}) collective-permute-start(bf16[64,1792]{1,0:T(8,128)(2,1)} %get-tuple-element.41), channel_id=1, source_target_pairs={{0,8},{4,12},{8,0},{12,4},{16,24},{20,28},{24,16},{28,20},{1,9},{5... | collective-permute-start | bytes 688136 | tf_op jit(solution)/shard_map/ppermute | solution.py:13
  7.4 11.5 %collective-permute-start.4 = (bf16[64,1792]{1,0:T(8,128)(2,1)}, bf16[64,1792]{1,0:T(8,128)(2,1)S(1)}, u32[]{:S(2)}, u32[]{:S(2)}) collective-permute-start(bf16[64,1792]{1,0:T(8,128)(2,1)} %get-tuple-element.42), channel_id=1, source_target_pairs={{0,24},{4,28},{8,16},{12,20},{16,8},{20,12},{24,0},{28,4},{1,25},{... | collective-permute-start | bytes 688136 | tf_op jit(solution)/shard_map/ppermute | solution.py:13
  7.4 22.8 %collective-permute-start.6 = (bf16[2,2,32,1024]{3,2,1,0:T(8,128)(2,1)}, bf16[2,2,32,1024]{3,2,1,0:T(8,128)(2,1)S(1)}, u32[]{:S(2)}, u32[]{:S(2)}) collective-permute-start(bf16[2,2,32,1024]{3,2,1,0:T(8,128)(2,1)} %bitcast.74), channel_id=1, source_target_pairs={{0,1},{3,2},{4,5},{7,6},{8,9},{11,10},{12,13},{15,14},{16,17},{19,... | collective-permute-start | bytes 786440 | tf_op jit(solution)/shard_map/ppermute | solution.py:260
  19.0 19.6 %collective-permute-start.8 = (bf16[128,1792]{1,0:T(8,128)(2,1)S(1)}, bf16[128,1792]{1,0:T(8,128)(2,1)S(1)}, u32[]{:S(2)}, u32[]{:S(2)}) collective-permute-start(bf16[128,1792]{1,0:T(8,128)(2,1)S(1)} %pad_maximum_fusion.2), channel_id=1, source_target_pairs={{0,4},{4,0},{8,12},{12,8},{16,20},{20,16},{24,28},{28,24},{1,5},{5... | collective-permute-start | bytes 1376264 | tf_op jit(solution)/shard_map/ppermute | solution.py:13
  20.5 8.8 %collective-permute-start.1 = (bf16[64,2048]{1,0:T(8,128)(2,1)S(1)}, bf16[64,2048]{1,0:T(8,128)(2,1)S(1)}, u32[]{:S(2)}, u32[]{:S(2)}) collective-permute-start(bf16[64,2048]{1,0:T(8,128)(2,1)S(1)} %convolution_convert_fusion.9), channel_id=1, source_target_pairs={{0,1},{3,2},{4,5},{7,6},{8,9},{11,10},{12,13},{15,14},{16,17},{19,... | collective-permute-start | bytes 786440 | tf_op jit(solution)/shard_map/ppermute | solution.py:317
  29.4 8.2 %collective-permute-start.2 = (bf16[32,2048]{1,0:T(8,128)(2,1)S(1)}, bf16[32,2048]{1,0:T(8,128)(2,1)S(1)}, u32[]{:S(2)}, u32[]{:S(2)}) collective-permute-start(bf16[32,2048]{1,0:T(8,128)(2,1)S(1)} %broadcast_select_fusion.9), channel_id=1, source_target_pairs={{0,0},{1,2},{2,1},{3,3},{4,4},{5,6},{6,5},{7,7},{8,8},{9,10},{10,9... | collective-permute-start | bytes 393224 | tf_op jit(solution)/shard_map/ppermute | solution.py:327
  30.1 9.7 %collective-permute-start.13 = (bf16[128,1792]{1,0:T(8,128)(2,1)S(1)}, bf16[128,1792]{1,0:T(8,128)(2,1)S(1)}, u32[]{:S(2)}, u32[]{:S(2)}) collective-permute-start(bf16[128,1792]{1,0:T(8,128)(2,1)S(1)} %pad_maximum_fusion.4), channel_id=1, source_target_pairs={{0,4},{4,0},{8,12},{12,8},{16,20},{20,16},{24,28},{28,24},{1,5},{5... | collective-permute-start | bytes 1376264 | tf_op jit(solution)/shard_map/ppermute | solution.py:13
  30.4 24.8 %collective-permute-start.5 = (bf16[128,2048]{1,0:T(8,128)(2,1)S(1)}, bf16[128,2048]{1,0:T(8,128)(2,1)S(1)}, u32[]{:S(2)}, u32[]{:S(2)}) collective-permute-start(bf16[128,2048]{1,0:T(8,128)(2,1)S(1)} %convolution_convert_fusion.5), channel_id=1, source_target_pairs={{0,1},{3,2},{4,5},{7,6},{8,9},{11,10},{12,13},{15,14},{16,17},{19,... | collective-permute-start | bytes 1572872 | tf_op jit(solution)/shard_map/ppermute | solution.py:317
  37.8 4.6 %collective-permute-start.10 = (bf16[32,2048]{1,0:T(8,128)(2,1)S(1)}, bf16[32,2048]{1,0:T(8,128)(2,1)S(1)}, u32[]{:S(2)}, u32[]{:S(2)}) collective-permute-start(bf16[32,2048]{1,0:T(8,128)(2,1)S(1)} %pad_maximum_fusion.19), channel_id=1, source_target_pairs={{0,0},{1,2},{2,1},{3,3},{4,4},{5,6},{6,5},{7,7},{8,8},{9,10},{10,9... | collective-permute-start | bytes 393224 | tf_op jit(solution)/shard_map/ppermute | solution.py:361
  42.5 10.3 %collective-permute-start.12 = (bf16[64,2048]{1,0:T(8,128)(2,1)S(1)}, bf16[64,2048]{1,0:T(8,128)(2,1)S(1)}, u32[]{:S(2)}, u32[]{:S(2)}) collective-permute-start(bf16[64,2048]{1,0:T(8,128)(2,1)S(1)} %maximum_select_fusion.3), channel_id=1, source_target_pairs={{1,0},{2,3},{5,4},{6,7},{9,8},{10,11},{13,12},{14,15},{17,16},{18,... | collective-permute-start | bytes 786440 | tf_op jit(solution)/shard_map/ppermute | solution.py:369
  55.3 3.9 %collective-permute-start.7 = (bf16[64,2048]{1,0:T(8,128)(2,1)S(1)}, bf16[64,2048]{1,0:T(8,128)(2,1)S(1)}, u32[]{:S(2)}, u32[]{:S(2)}) collective-permute-start(bf16[64,2048]{1,0:T(8,128)(2,1)S(1)} %broadcast_select_fusion.7), channel_id=1, source_target_pairs={{0,0},{1,2},{2,1},{3,3},{4,4},{5,6},{6,5},{7,7},{8,8},{9,10},{10,9... | collective-permute-start | bytes 786440 | tf_op jit(solution)/shard_map/ppermute | solution.py:327
  56.0 11.9 %collective-permute-start.9 = (bf16[128,2048]{1,0:T(8,128)(2,1)S(1)}, bf16[128,2048]{1,0:T(8,128)(2,1)S(1)}, u32[]{:S(2)}, u32[]{:S(2)}) collective-permute-start(bf16[128,2048]{1,0:T(8,128)(2,1)S(1)} %convolution_convert_fusion.4), channel_id=1, source_target_pairs={{0,1},{3,2},{4,5},{7,6},{8,9},{11,10},{12,13},{15,14},{16,17},{19,... | collective-permute-start | bytes 1572872 | tf_op jit(solution)/shard_map/ppermute | solution.py:317
  59.5 9.3 %collective-permute-start.15 = (bf16[64,2048]{1,0:T(8,128)(2,1)S(1)}, bf16[64,2048]{1,0:T(8,128)(2,1)S(1)}, u32[]{:S(2)}, u32[]{:S(2)}) collective-permute-start(bf16[64,2048]{1,0:T(8,128)(2,1)S(1)} %pad_maximum_fusion.6), channel_id=1, source_target_pairs={{0,0},{1,2},{2,1},{3,3},{4,4},{5,6},{6,5},{7,7},{8,8},{9,10},{10,9... | collective-permute-start | bytes 786440 | tf_op jit(solution)/shard_map/ppermute | solution.py:361
  68.1 9.6 %collective-permute-start.11 = (bf16[64,2048]{1,0:T(8,128)(2,1)S(1)}, bf16[64,2048]{1,0:T(8,128)(2,1)S(1)}, u32[]{:S(2)}, u32[]{:S(2)}) collective-permute-start(bf16[64,2048]{1,0:T(8,128)(2,1)S(1)} %broadcast_select_fusion.6), channel_id=1, source_target_pairs={{0,0},{1,2},{2,1},{3,3},{4,4},{5,6},{6,5},{7,7},{8,8},{9,10},{10,9... | collective-permute-start | bytes 786440 | tf_op jit(solution)/shard_map/ppermute | solution.py:327
  68.9 15.2 %collective-permute-start.17 = (bf16[128,2048]{1,0:T(8,128)(2,1)S(1)}, bf16[128,2048]{1,0:T(8,128)(2,1)S(1)}, u32[]{:S(2)}, u32[]{:S(2)}) collective-permute-start(bf16[128,2048]{1,0:T(8,128)(2,1)S(1)} %maximum_select_fusion), channel_id=1, source_target_pairs={{1,0},{2,3},{5,4},{6,7},{9,8},{10,11},{13,12},{14,15},{17,16},{18,... | collective-permute-start | bytes 1572872 | tf_op jit(solution)/shard_map/ppermute | solution.py:369
  70.2 15.1 %collective-permute-start.14 = (bf16[128,2048]{1,0:T(8,128)(2,1)S(1)}, bf16[128,2048]{1,0:T(8,128)(2,1)S(1)}, u32[]{:S(2)}, u32[]{:S(2)}) collective-permute-start(bf16[128,2048]{1,0:T(8,128)(2,1)S(1)} %convolution_convert_fusion.3), channel_id=1, source_target_pairs={{0,1},{3,2},{4,5},{7,6},{8,9},{11,10},{12,13},{15,14},{16,17},{19,... | collective-permute-start | bytes 1572872 | tf_op jit(solution)/shard_map/ppermute | solution.py:317
  78.8 20.7 %collective-permute-start.21 = (bf16[128,2048]{1,0:T(8,128)(2,1)S(1)}, bf16[128,2048]{1,0:T(8,128)(2,1)S(1)}, u32[]{:S(2)}, u32[]{:S(2)}) collective-permute-start(bf16[128,2048]{1,0:T(8,128)(2,1)S(1)} %maximum_select_fusion.1), channel_id=1, source_target_pairs={{1,0},{2,3},{5,4},{6,7},{9,8},{10,11},{13,12},{14,15},{17,16},{18,... | collective-permute-start | bytes 1572872 | tf_op jit(solution)/shard_map/ppermute | solution.py:369
  85.5 11.9 %collective-permute-start.16 = (bf16[64,2048]{1,0:T(8,128)(2,1)S(1)}, bf16[64,2048]{1,0:T(8,128)(2,1)S(1)}, u32[]{:S(2)}, u32[]{:S(2)}) collective-permute-start(bf16[64,2048]{1,0:T(8,128)(2,1)S(1)} %broadcast_select_fusion.5), channel_id=1, source_target_pairs={{0,0},{1,2},{2,1},{3,3},{4,4},{5,6},{6,5},{7,7},{8,8},{9,10},{10,9... | collective-permute-start | bytes 786440 | tf_op jit(solution)/shard_map/ppermute | solution.py:327
  86.2 12.5 %collective-permute-start.18 = (bf16[64,2048]{1,0:T(8,128)(2,1)S(1)}, bf16[64,2048]{1,0:T(8,128)(2,1)S(1)}, u32[]{:S(2)}, u32[]{:S(2)}) collective-permute-start(bf16[64,2048]{1,0:T(8,128)(2,1)S(1)} %convolution_convert_fusion.7), channel_id=1, source_target_pairs={{0,1},{3,2},{4,5},{7,6},{8,9},{11,10},{12,13},{15,14},{16,17},{19,... | collective-permute-start | bytes 786440 | tf_op jit(solution)/shard_map/ppermute | solution.py:317
  97.7 5.4 %collective-permute-start.24 = (bf16[64,2048]{1,0:T(8,128)(2,1)S(1)}, bf16[64,2048]{1,0:T(8,128)(2,1)S(1)}, u32[]{:S(2)}, u32[]{:S(2)}) collective-permute-start(bf16[64,2048]{1,0:T(8,128)(2,1)S(1)} %pad_maximum_fusion.8), channel_id=1, source_target_pairs={{0,0},{1,2},{2,1},{3,3},{4,4},{5,6},{6,5},{7,7},{8,8},{9,10},{10,9... | collective-permute-start | bytes 786440 | tf_op jit(solution)/shard_map/ppermute | solution.py:361
  102.3 6.7 %collective-permute-start.22 = (bf16[32,2048]{1,0:T(8,128)(2,1)S(1)}, bf16[32,2048]{1,0:T(8,128)(2,1)S(1)}, u32[]{:S(2)}, u32[]{:S(2)}) collective-permute-start(bf16[32,2048]{1,0:T(8,128)(2,1)S(1)} %pad_maximum_fusion.23), channel_id=1, source_target_pairs={{0,0},{1,2},{2,1},{3,3},{4,4},{5,6},{6,5},{7,7},{8,8},{9,10},{10,9... | collective-permute-start | bytes 393224 | tf_op jit(solution)/shard_map/ppermute | solution.py:361
  103.2 19.8 %collective-permute-start.25 = (bf16[128,2048]{1,0:T(8,128)(2,1)S(1)}, bf16[128,2048]{1,0:T(8,128)(2,1)S(1)}, u32[]{:S(2)}, u32[]{:S(2)}) collective-permute-start(bf16[128,2048]{1,0:T(8,128)(2,1)S(1)} %maximum_select_fusion.2), channel_id=1, source_target_pairs={{1,0},{2,3},{5,4},{6,7},{9,8},{10,11},{13,12},{14,15},{17,16},{18,... | collective-permute-start | bytes 1572872 | tf_op jit(solution)/shard_map/ppermute | solution.py:369
  104.5 23.5 %collective-permute-start.27 = (bf16[64,1792]{1,0:T(8,128)(2,1)S(1)}, bf16[64,1792]{1,0:T(8,128)(2,1)S(1)}, u32[]{:S(2)}, u32[]{:S(2)}) collective-permute-start(bf16[64,1792]{1,0:T(8,128)(2,1)S(1)} %pad_maximum_fusion.13), channel_id=1, source_target_pairs={{0,8},{4,12},{8,0},{12,4},{16,24},{20,28},{24,16},{28,20},{1,9},{5... | collective-permute-start | bytes 688136 | tf_op jit(solution)/shard_map/ppermute | solution.py:13
  106.1 22.0 %collective-permute-start.28 = (bf16[64,1792]{1,0:T(8,128)(2,1)S(1)}, bf16[64,1792]{1,0:T(8,128)(2,1)S(1)}, u32[]{:S(2)}, u32[]{:S(2)}) collective-permute-start(bf16[64,1792]{1,0:T(8,128)(2,1)S(1)} %pad_maximum_fusion.14), channel_id=1, source_target_pairs={{0,24},{4,28},{8,16},{12,20},{16,8},{20,12},{24,0},{28,4},{1,25},{... | collective-permute-start | bytes 688136 | tf_op jit(solution)/shard_map/ppermute | solution.py:13
  107.7 15.4 %collective-permute-start.26 = (bf16[64,1792]{1,0:T(8,128)(2,1)S(1)}, bf16[64,1792]{1,0:T(8,128)(2,1)S(1)}, u32[]{:S(2)}, u32[]{:S(2)}) collective-permute-start(bf16[64,1792]{1,0:T(8,128)(2,1)S(1)} %pad_maximum_fusion.12), channel_id=1, source_target_pairs={{0,16},{4,20},{8,24},{12,28},{16,0},{20,4},{24,8},{28,12},{1,17},{... | collective-permute-start | bytes 688136 | tf_op jit(solution)/shard_map/ppermute | solution.py:13
  109.1 19.0 %collective-permute-start.23 = (bf16[64,2048]{1,0:T(8,128)(2,1)S(1)}, bf16[64,2048]{1,0:T(8,128)(2,1)S(1)}, u32[]{:S(2)}, u32[]{:S(2)}) collective-permute-start(bf16[64,2048]{1,0:T(8,128)(2,1)S(1)} %maximum_select_fusion.4), channel_id=1, source_target_pairs={{1,0},{2,3},{5,4},{6,7},{9,8},{10,11},{13,12},{14,15},{17,16},{18,... | collective-permute-start | bytes 786440 | tf_op jit(solution)/shard_map/ppermute | solution.py:369
  130.5 20.7 %collective-permute-start.29 = (bf16[2,2,32,1024]{3,2,1,0:T(8,128)(2,1)S(1)}, bf16[2,2,32,1024]{3,2,1,0:T(8,128)(2,1)S(1)}, u32[]{:S(2)}, u32[]{:S(2)}) collective-permute-start(bf16[2,2,32,1024]{3,2,1,0:T(8,128)(2,1)S(1)} %slice_bitcast_fusion), channel_id=1, source_target_pairs={{1,0},{2,3},{5,4},{6,7},{9,8},{10,11},{13,12},{14,15},{17,16},{18,... | collective-permute-start | bytes 786440 | tf_op jit(solution)/shard_map/ppermute | solution.py:396
  131.8 10.2 %collective-permute-start.30 = (bf16[64,1792]{1,0:T(8,128)(2,1)S(1)}, bf16[64,1792]{1,0:T(8,128)(2,1)S(1)}, u32[]{:S(2)}, u32[]{:S(2)}) collective-permute-start(bf16[64,1792]{1,0:T(8,128)(2,1)S(1)} %pad_maximum_fusion.15), channel_id=1, source_target_pairs={{0,12},{4,8},{8,4},{12,0},{16,28},{20,24},{24,20},{28,16},{1,13},{... | collective-permute-start | bytes 688136 | tf_op jit(solution)/shard_map/ppermute | solution.py:13
  131.9 14.4 %collective-permute-start.31 = (bf16[64,1792]{1,0:T(8,128)(2,1)S(1)}, bf16[64,1792]{1,0:T(8,128)(2,1)S(1)}, u32[]{:S(2)}, u32[]{:S(2)}) collective-permute-start(bf16[64,1792]{1,0:T(8,128)(2,1)S(1)} %pad_maximum_fusion.16), channel_id=1, source_target_pairs={{0,28},{4,24},{8,20},{12,16},{16,12},{20,8},{24,4},{28,0},{1,29},{... | collective-permute-start | bytes 688136 | tf_op jit(solution)/shard_map/ppermute | solution.py:13
  135.3 11.0 %collective-permute-start.32 = (bf16[64,1792]{1,0:T(8,128)(2,1)S(1)}, bf16[64,1792]{1,0:T(8,128)(2,1)S(1)}, u32[]{:S(2)}, u32[]{:S(2)}) collective-permute-start(bf16[64,1792]{1,0:T(8,128)(2,1)S(1)} %pad_maximum_fusion.17), channel_id=1, source_target_pairs={{0,4},{4,0},{8,12},{12,8},{16,20},{20,16},{24,28},{28,24},{1,5},{5... | collective-permute-start | bytes 688136 | tf_op jit(solution)/shard_map/ppermute | solution.py:13
  135.4 12.3 %collective-permute-start.33 = (bf16[64,1792]{1,0:T(8,128)(2,1)S(1)}, bf16[64,1792]{1,0:T(8,128)(2,1)S(1)}, u32[]{:S(2)}, u32[]{:S(2)}) collective-permute-start(bf16[64,1792]{1,0:T(8,128)(2,1)S(1)} %pad_maximum_fusion.18), channel_id=1, source_target_pairs={{0,20},{4,16},{8,28},{12,24},{16,4},{20,0},{24,12},{28,8},{1,21},{... | collective-permute-start | bytes 688136 | tf_op jit(solution)/shard_map/ppermute | solution.py:13
  (11 other events, 61.4 us)
